TPU v7x, 32 devices: a whole 2x2x4 slice. The times are simulated.
32 devices in a mesh: own: 2 (over y), space: 16 (over z, x, core).
Axes of the slice: x: 2, y: 2, z: 4, core: 2. Of those that a mesh axis runs over, the one named last changes fastest.
Arguments:
- density: bfloat16 [256, 4, 64, 128], P(None, 'own', 'space'), may hold values from -6 to 6
- cotangent: bfloat16 [256, 4, 64, 128], P(None, 'own', 'space'), may hold values from -6 to 6
- pw_one: bfloat16 [256, 256], P('own'), may hold values from -0.375 to 0.375
- pw_two: bfloat16 [256, 256], P('own'), may hold values from -0.375 to 0.375
- dw_one: bfloat16 [27, 256], P(None, 'own'), may hold values from -1.25 to 1.25
- dw_two: bfloat16 [27, 256], P(None, 'own'), may hold values from -1.25 to 1.25
Outputs:
- grad_input: bfloat16 [256, 4, 64, 128], P(None, 'own', 'space')
- grad_pw_one: float32 [256, 256], P('own')
- grad_pw_two: float32 [256, 256], P('own')
- grad_dw_one: float32 [27, 256], P(None, 'own')
- grad_dw_two: float32 [27, 256], P(None, 'own')
All inputs are finite; a program needn't handle non-finite values.
Results may differ from a plain program's by a relative error of at most 0.01.
Values may be sent and summed in bfloat16 or wider, within the bound.
No kernel may reach another device: no remote copies, remote signals or barrier semaphores. Data moves between devices by JAX's collectives and lax.ppermute only.
A program may use at most 192 MiB of HBM per device.

v0:
```python
import math

import jax
import jax.numpy as jnp
from jax import lax
from jax.sharding import PartitionSpec as P

TAP_LIST = [
    (9 * (a + 1) + 3 * (b + 1) + (d + 1), a, b, d)
    for a in (-1, 0, 1)
    for b in (-1, 0, 1)
    for d in (-1, 0, 1)
]


def extended(value, sides, width):
    for axis, dim in sides:
        size, length = (lax.axis_size(axis), value.shape[dim])
        up = [(i, (i + 1) % size) for i in range(size)]
        down = [(j, i) for i, j in up]
        last = lax.slice_in_dim(value, length - width, length, axis=dim)
        first = lax.slice_in_dim(value, 0, width, axis=dim)
        before = lax.ppermute(last, axis, up)
        after = lax.ppermute(first, axis, down)
        value = jnp.concatenate([before, value, after], axis=dim)
    return value


def depthwise(padded, weights, extent_x, extent_y, direction):
    running = jnp.zeros((padded.shape[0], extent_x, extent_y, padded.shape[3]), jnp.float32)
    for k, a, b, d in TAP_LIST:
        start_x = 1 + direction * a
        start_y = 1 + direction * b
        shifted = padded[:, start_x : start_x + extent_x, start_y : start_y + extent_y, :]
        shifted = jnp.roll(shifted, -direction * d, axis=3).astype(jnp.float32)
        running = running + weights[k].astype(jnp.float32)[:, None, None, None] * shifted
    return running


def tap_sums(padded, gradient):
    extent_x = gradient.shape[1]
    extent_y = gradient.shape[2]
    grad_float = gradient.astype(jnp.float32)
    columns = []
    for k, a, b, d in TAP_LIST:
        shifted = padded[:, 1 + a : 1 + a + extent_x, 1 + b : 1 + b + extent_y, :]
        shifted = jnp.roll(shifted, -d, axis=3).astype(jnp.float32)
        columns.append(jnp.sum(shifted * grad_float, axis=(1, 2, 3)))
    return jnp.stack(columns, axis=0)


def pointwise(weights, source):
    layout = source.shape
    flattened = source.reshape(layout[0], -1)
    return jnp.dot(weights.T, flattened, preferred_element_type=jnp.float32).reshape(layout)


def backmap(weights, source):
    layout = source.shape
    flattened = source.reshape(layout[0], -1)
    return jnp.dot(weights, flattened, preferred_element_type=jnp.float32).reshape(layout)


def contract_cells(left, right):
    channels = left.shape[0]
    return lax.dot_general(
        left.reshape(channels, -1),
        right.reshape(channels, -1),
        (((1,), (1,)), ((), ())),
        preferred_element_type=jnp.float32,
    )


def shards(density, cotangent, pw_one, pw_two, dw_one, dw_two):
    channels, extent_x, extent_y, extent_z = density.shape
    weight_one, weight_two, taps_one, taps_two = (
        lax.all_gather(pw_one, "own", axis=0, tiled=True),
        lax.all_gather(pw_two, "own", axis=0, tiled=True),
        lax.all_gather(dw_one, "own", axis=1, tiled=True),
        lax.all_gather(dw_two, "own", axis=1, tiled=True),
    )
    rim_width = 1
    wide_input = extended(density, (("own", 1), ("space", 2)), rim_width)
    first = depthwise(wide_input, taps_one, extent_x, extent_y, 1).astype(jnp.bfloat16)
    pre = pointwise(weight_one, first)
    act = jax.nn.silu(pre).astype(jnp.bfloat16)
    act_padded = extended(act, (("own", 1), ("space", 2)), 1)
    second = depthwise(act_padded, taps_two, extent_x, extent_y, 1).astype(jnp.bfloat16)
    grad_second = backmap(weight_two, cotangent).astype(jnp.bfloat16)
    second_padded = extended(grad_second, (("own", 1), ("space", 2)), 1)
    sigma = jax.nn.sigmoid(pre)
    grad_pre = (
        depthwise(second_padded, taps_two, extent_x, extent_y, -1)
        * (sigma * (1.0 + pre * (1.0 - sigma)))
    ).astype(jnp.bfloat16)
    grad_first = backmap(weight_one, grad_pre).astype(jnp.bfloat16)
    first_padded = extended(grad_first, (("own", 1), ("space", 2)), 1)
    grad_input = (
        cotangent.astype(jnp.float32) + depthwise(first_padded, taps_one, extent_x, extent_y, -1)
    ).astype(jnp.bfloat16)
    total_cells = extent_x * extent_y * extent_z * lax.axis_size("own") * lax.axis_size("space")
    grad_scale = 1.0 / math.sqrt(float(total_cells))
    local_pw_one = contract_cells(first, grad_pre) * grad_scale
    local_pw_two = contract_cells(second, cotangent) * grad_scale
    local_dw_one = tap_sums(wide_input, grad_first) * grad_scale
    local_dw_two = tap_sums(act_padded, grad_second) * grad_scale
    partials = (local_pw_one, local_pw_two, local_dw_one, local_dw_two)
    summed = lax.psum((partials[0], partials[1], partials[2], partials[3]), ("own", "space"))
    share_rows = channels // lax.axis_size("own")
    position = lax.axis_index("own") * share_rows
    result = (
        lax.dynamic_slice_in_dim(summed[0], position, share_rows, 0),
        lax.dynamic_slice_in_dim(summed[1], position, share_rows, 0),
        lax.dynamic_slice_in_dim(summed[2], position, share_rows, 1),
        lax.dynamic_slice_in_dim(summed[3], position, share_rows, 1),
    )
    return (grad_input, result[0], result[1], result[2], result[3])


def solution(mesh):
    in_specs = (
        P(None, "own", "space", None),
        P(None, "own", "space", None),
        P("own", None),
        P("own", None),
        P(None, "own"),
        P(None, "own"),
    )
    out_specs = (
        P(None, "own", "space", None),
        P("own", None),
        P("own", None),
        P(None, "own"),
        P(None, "own"),
    )
    return jax.shard_map(shards, mesh=mesh, in_specs=in_specs, out_specs=out_specs, check_vma=False)
```

profile of v0, /device:TPU:0, one launch (start us, length us, event | category | flops | bytes accessed | tf_op | source)
XLA Modules:
  0.0 316.8 jit_solution(11550276840240221718)
XLA Ops:
  7.3 1.4 copy.90
  8.7 3.0 collective-permute-start.5
  11.8 12.0 %all_gather.12 = bf16[27,256]{1,0:T(8,128)(2,1)S(1)} all-gather(bf16[27,128]{1,0:T(8,128)(2,1)S(1)} %copy-done.80), channel_id=1, replica_groups=mesh['own'=2,'space'=16] {'own'}, dimensions={1}, use_global_device_ids=true | all-gather | bytes 20736 | tf_op jit(solution)/shard_map/all_gather | solution.py:79
  25.1 4.3 %all_gather.13 = bf16[27,256]{1,0:T(8,128)(2,1)S(1)} all-gather(bf16[27,128]{1,0:T(8,128)(2,1)S(1)} %copy-done.81), channel_id=1, replica_groups=mesh['own'=2,'space'=16] {'own'}, dimensions={1}, use_global_device_ids=true | all-gather | bytes 20736 | tf_op jit(solution)/shard_map/all_gather | solution.py:80
  30.8 4.9 %all_gather.15 = bf16[256,256]{1,0:T(8,128)(2,1)S(1)} all-gather(bf16[128,256]{1,0:T(8,128)(2,1)S(1)} %copy-done.24), channel_id=1, replica_groups=mesh['own'=2,'space'=16] {'own'}, dimensions={0}, use_global_device_ids=true | all-gather | bytes 196608 | tf_op jit(solution)/shard_map/all_gather | solution.py:77
  36.1 1.1 copy.88
  37.2 1.0 copy.89
  38.2 5.0 %all_gather.14 = bf16[256,256]{1,0:T(8,128)(2,1)} all-gather(bf16[128,256]{1,0:T(8,128)(2,1)S(1)} %copy-done.25), channel_id=1, replica_groups=mesh['own'=2,'space'=16] {'own'}, dimensions={0}, use_global_device_ids=true | all-gather | bytes 196608 | tf_op jit(solution)/shard_map/all_gather | solution.py:78
  43.6 0.9 copy.96
  44.5 4.4 %collective-permute-start.7 = (bf16[256,4,1,128]{3,0,2,1:T(8,128)(2,1)}, bf16[256,4,1,128]{3,0,2,1:T(8,128)(2,1)}, u32[]{:S(2)}, u32[]{:S(2)}) collective-permute-start(bf16[256,4,1,128]{3,0,2,1:T(8,128)(2,1)} %copy.96), channel_id=1, source_target_pairs={{1,0},{2,1},{3,2},{4,3},{5,4},{6,5},{7,6},{8,7},{9,8},{10,9},{11,1... | collective-permute-start | bytes 786440 | tf_op jit(solution)/shard_map/ppermute | solution.py:24
  48.9 1.4 fusion.146
  50.3 2.3 fusion.217
  52.7 1.8 copy.94
  54.5 1.8 copy.97
  56.2 1.2 maximum_maximum_fusion.1
  57.8 1.8 fusion.289
  60.0 11.0 %add_convert_fusion = (bf16[256,2,4,128]{0,3,2,1:T(8,128)(2,1)S(1)}, f32[256,2,4,128]{0,3,2,1:T(8,128)}, f32[256,2,4,128]{0,3,2,1:T(8,128)}, f32[256,2,4,128]{0,...) fusion(bf16[256,2,4,128]{0,3,2,1:T(8,128)(2,1)S(1)} %copy.90, ...), kind=kLoop, calls=%fused_computation.272 | loop fusion | flops 57933824 | bytes 27225088 | tf_op jit(solution)/shard_map/convert_element_type | solution.py:84
  72.3 1.8 collective-permute-start.13
  74.3 1.5 maximum_convert_fusion
  75.9 5.5 %collective-permute-done.13 = bf16[256,1,4,128]{0,3,2,1:T(8,128)(2,1)S(1)} collective-permute-done((bf16[256,1,4,128]{0,3,2,1:T(8,128)(2,1)S(1)}, bf16[256,1,4,128]{0,3,2,1:T(8,128)(2,1)S(1)}, u32[]{:S(2)}, u32[]{:S(2)}) %collective-permute-start.13) | collective-permute-done | bytes 262176 | tf_op jit(solution)/shard_map/ppermute | solution.py:24
  81.4 5.1 %collective-permute-done.12 = bf16[256,1,4,128]{0,3,2,1:T(8,128)(2,1)S(1)} collective-permute-done((bf16[256,1,4,128]{0,3,2,1:T(8,128)(2,1)S(1)}, bf16[256,1,4,128]{0,3,2,1:T(8,128)(2,1)S(1)}, u32[]{:S(2)}, u32[]{:S(2)}) %collective-permute-start.12) | collective-permute-done | bytes 262176 | tf_op jit(solution)/shard_map/ppermute | solution.py:23
  86.6 4.4 %collective-permute-start.15 = (bf16[256,4,1,128]{0,3,2,1:T(8,128)(2,1)S(1)}, bf16[256,4,1,128]{0,3,2,1:T(8,128)(2,1)S(1)}, u32[]{:S(2)}, u32[]{:S(2)}) collective-permute-start(bf16[256,4,1,128]{0,3,2,1:T(8,128)(2,1)S(1)} %get-tuple-element.148), channel_id=1, source_target_pairs={{1,0},{2,1},{3,2},{4,3},{5,4},{6,5},{7,6},{8,7},{9,8},{10,9},{11,1... | collective-permute-start | bytes 786440 | tf_op jit(solution)/shard_map/ppermute | solution.py:24
  91.5 3.7 %collective-permute-done.14 = bf16[256,4,1,128]{0,3,2,1:T(8,128)(2,1)S(1)} collective-permute-done((bf16[256,4,1,128]{0,3,2,1:T(8,128)(2,1)S(1)}, bf16[256,4,1,128]{0,3,2,1:T(8,128)(2,1)S(1)}, u32[]{:S(2)}, u32[]{:S(2)}) %collective-permute-start.14) | collective-permute-done | bytes 262176 | tf_op jit(solution)/shard_map/ppermute | solution.py:23
  96.5 2.1 fusion.120
  99.4 1.7 collective-permute-start
  102.2 1.4 fusion.135
  103.5 1.3 fusion.131
  105.1 2.1 fusion.136
  107.4 5.8 %fusion = f32[256,256]{1,0:T(8,128)} fusion(bf16[256,2,4,128]{0,3,2,1:T(8,128)(2,1)S(1)} %copy-done.11, bf16[256,2,4,128]{0,3,2,1:T(8,128)(2,1)S(1)} %multiply_convert_fusion, f32[256]{0:T(256)S(1)} %bitcast.317, f32[256]{0:T(256)S(1)} %bitcast.319, f32[256]{0:T(256)S(1)} %bitcast.321, f32[256]{0:T(256)S(1)} %bitcast.323, f32[256]{0:T(256)S(1)} %bitcast.325, ...), kind=kOutput, calls=%fused_computation.119 | convolution fusion | flops 192217088 | bytes 14986240 | tf_op jit(solution)/shard_map/dot_general | solution.py:66
  113.2 1.2 fusion.137
  114.4 5.2 %stack.223 = f32[27,256]{1,0:T(8,128)} concatenate(f32[1,256]{1,0:T(1,128)} %bitcast.379, f32[1,256]{1,0:T(1,128)} %bitcast.306, f32[1,256]{1,0:T(1,128)} %bitcast.380, f32[1,256]{1,0:T(1,128)} %bitcast.309, f32[1,256]{1,0:T(1,128)} %bitcast.381, f32[1,256]{1,0:T(1,128)} %bitcast.310, f32[1,256]{1,0:T(1,128)S(1)} %bitcast.275, f32[1,256]{1,0:T(1,128)} %bitcast.303, ...), dimensions={0} | concatenate | bytes 55296 | tf_op jit(solution)/shard_map/stack | solution.py:49
  119.6 1.4 broadcast_multiply_fusion
  121.1 4.4 %collective-permute-start.2 = (bf16[256,4,1,128]{0,3,2,1:T(8,128)(2,1)S(1)}, bf16[256,4,1,128]{0,3,2,1:T(8,128)(2,1)S(1)}, u32[]{:S(2)}, u32[]{:S(2)}) collective-permute-start(bf16[256,4,1,128]{0,3,2,1:T(8,128)(2,1)S(1)} %get-tuple-element.155), channel_id=1, source_target_pairs={{1,0},{2,1},{3,2},{4,3},{5,4},{6,5},{7,6},{8,7},{9,8},{10,9},{11,1... | collective-permute-start | bytes 786440 | tf_op jit(solution)/shard_map/ppermute | solution.py:24
  126.1 3.7 %collective-permute-done.3 = bf16[256,4,1,128]{0,3,2,1:T(8,128)(2,1)S(1)} collective-permute-done((bf16[256,4,1,128]{0,3,2,1:T(8,128)(2,1)S(1)}, bf16[256,4,1,128]{0,3,2,1:T(8,128)(2,1)S(1)}, u32[]{:S(2)}, u32[]{:S(2)}) %collective-permute-start.3) | collective-permute-done | bytes 262176 | tf_op jit(solution)/shard_map/ppermute | solution.py:23
  132.2 9.1 %fusion.139 = bf16[256,2,4,128]{0,3,2,1:T(8,128)(2,1)S(1)} fusion(f32[256,2,4,128]{0,3,2,1:T(8,128)S(1)} %bitcast.215, bf16[256,2,4,128]{0,3,2,1:T(8,128)(2,1)S(1)} %get-tuple-element.274, bf16[256,1,4,128]{0,3,2,1:T(8,128)(2,1)S(1)} %collective-permute-done, bf16[256,1,4,128]{0,3,2,1:T(8,128)(2,1)S(1)} %collective-permute-done.1, ...), kind=kLoop, calls=%fused_computation.274 | loop fusion | flops 58982400 | bytes 14666752 | tf_op jit(solution)/shard_map/convert_element_type | solution.py:95
  142.1 1.1 fusion.1
  143.1 8.2 %fusion.95 = (f32[256]{0:T(256)S(1)}, f32[256]{0:T(256)S(1)}, f32[256]{0:T(256)S(1)}, f32[256]{0:T(256)S(1)}, f32[256]{0:T(256)}, /*index=5*/f32[256]{0:T(256)},...) fusion(f32[256,2,4,128]{0,3,2,1:T(8,128)} %get-tuple-element.96, ...), kind=kOutput, calls=%fused_computation.227 | convolution fusion | flops 144174592 | bytes 20072448 | tf_op jit(solution)/shard_map/dot_general | solution.py:61
  152.2 1.7 collective-permute-start.8
  154.4 2.3 fusion.77
  156.9 42.9 %all-reduce = (f32[27,256]{1,0:T(8,128)S(1)}, f32[27,256]{1,0:T(8,128)S(1)}) all-reduce(f32[27,256]{1,0:T(8,128)S(1)} %broadcast_multiply_fusion.1, f32[27,256]{1,0:T(8,128)S(1)} %copy-done.23), channel_id=1, replica_groups=mesh['own'=2,'space'=16] {'own','space'}, use_global_device_ids=true, to_apply=%region_29.30 | all-reduce | flops 13824 | bytes 110592 | tf_op jit(solution)/shard_map/psum | solution.py:108
  201.1 82.2 %all-reduce.4.cloned.1.call-done = (f32[256,256]{1,0:T(8,128)}, f32[256,256]{1,0:T(8,128)}) async-done(((f32[256,256]{1,0:T(8,128)}, f32[256,256]{1,0:T(8,128)}), (f32[256,256]{1,0:T(8,128)}, f32[256,256]{1,0:T(8,128)})) %all-reduce.4.cloned.1.call-update) | async-done | bytes 524304 | tf_op jit(solution)/shard_map/psum | solution.py:108
  283.3 1.6 constant_dynamic-slice_fusion.3
  284.9 1.6 constant_dynamic-slice_fusion.2
  286.9 4.7 %collective-permute-start.10 = (bf16[256,4,1,128]{3,0,2,1:T(8,128)(2,1)S(1)}, bf16[256,4,1,128]{3,0,2,1:T(8,128)(2,1)S(1)}, u32[]{:S(2)}, u32[]{:S(2)}) collective-permute-start(bf16[256,4,1,128]{3,0,2,1:T(8,128)(2,1)S(1)} %copy.104), channel_id=1, source_target_pairs={{1,0},{2,1},{3,2},{4,3},{5,4},{6,5},{7,6},{8,7},{9,8},{10,9},{11,1... | collective-permute-start | bytes 786440 | tf_op jit(solution)/shard_map/ppermute | solution.py:24
  291.7 1.6 fusion.152
  293.3 2.0 collective-permute-done.11
  298.4 9.5 %fusion.138 = bf16[256,2,4,128]{0,3,2,1:T(8,128)(2,1)} fusion(bf16[256,2,4,128]{0,3,2,1:T(8,128)(2,1)S(1)} %bitcast.213, bf16[256,2,4,128]{0,3,2,1:T(8,128)(2,1)S(1)} %copy-done.12, bf16[256,1,4,128]{0,3,2,1:T(8,128)(2,1)S(1)} %collective-permute-done.8, bf16[256,1,4,128]{0,3,2,1:T(8,128)(2,1)S(1)} %collective-permute-done.9, ...), kind=kLoop, calls=%fused_computation.273 | loop fusion | flops 57409536 | bytes 14142464 | tf_op jit(solution)/shard_map/convert_element_type | solution.py:100
  307.9 2.1 copy.112
  (360 shorter events, 17.9 us)
Async XLA Ops:
  7.2 4.6 %copy-start.80 = (bf16[27,128]{1,0:T(8,128)(2,1)S(1)}, bf16[27,128]{1,0:T(8,128)(2,1)}, u32[]{:S(2)}) copy-start(bf16[27,128]{1,0:T(8,128)(2,1)} %param.10) | copy-start | bytes 20740
  7.2 17.9 %copy-start.81 = (bf16[27,128]{1,0:T(8,128)(2,1)S(1)}, bf16[27,128]{1,0:T(8,128)(2,1)}, u32[]{:S(2)}) copy-start(bf16[27,128]{1,0:T(8,128)(2,1)} %param.11) | copy-start | bytes 20740
  7.2 23.6 %copy-start.24 = (bf16[128,256]{1,0:T(8,128)(2,1)S(1)}, bf16[128,256]{1,0:T(8,128)(2,1)}, u32[]{:S(2)}) copy-start(bf16[128,256]{1,0:T(8,128)(2,1)} %param.8) | copy-start | bytes 196612
  7.2 28.5 %copy-start.18 = (bf16[256,2,4,128]{3,2,1,0:T(4,128)(2,1)S(1)}, bf16[256,2,4,128]{3,2,1,0:T(4,128)(2,1)}, u32[]{:S(2)}) copy-start(bf16[256,2,4,128]{3,2,1,0:T(4,128)(2,1)} %param.7) | copy-start | bytes 1572868
  7.2 276.1 %all-reduce.4.cloned.1.call-start = ((), (), s32[]{:S(2)}) async-start(), calls=%async_computation | async-start | bytes 1048576 | tf_op jit(solution)/shard_map/psum | solution.py:108
  8.7 34.6 %collective-permute-start.5 = (bf16[256,1,4,128]{0,3,2,1:T(8,128)(2,1)S(1)}, bf16[256,1,4,128]{0,3,2,1:T(8,128)(2,1)S(1)}, u32[]{:S(2)}, u32[]{:S(2)}) collective-permute-start(bf16[256,1,4,128]{0,3,2,1:T(8,128)(2,1)S(1)} %get-tuple-element.218), channel_id=1, source_target_pairs={{16,0},{0,16},{17,1},{1,17},{18,2},{2,18},{19,3},{3,19},{20,4},{4,... | collective-permute-start | bytes 786440 | tf_op jit(solution)/shard_map/ppermute | solution.py:24
  11.7 31.6 %collective-permute-start.4 = (bf16[256,1,4,128]{0,3,2,1:T(8,128)(2,1)S(1)}, bf16[256,1,4,128]{0,3,2,1:T(8,128)(2,1)S(1)}, u32[]{:S(2)}, u32[]{:S(2)}) collective-permute-start(bf16[256,1,4,128]{0,3,2,1:T(8,128)(2,1)S(1)} %get-tuple-element.217), channel_id=1, source_target_pairs={{0,16},{16,0},{1,17},{17,1},{2,18},{18,2},{3,19},{19,3},{4,20},{20... | collective-permute-start | bytes 786440 | tf_op jit(solution)/shard_map/ppermute | solution.py:23
  43.6 9.1 %collective-permute-start.6 = (bf16[256,4,1,128]{3,0,2,1:T(8,128)(2,1)S(1)}, bf16[256,4,1,128]{3,0,2,1:T(8,128)(2,1)}, u32[]{:S(2)}, u32[]{:S(2)}) collective-permute-start(bf16[256,4,1,128]{3,0,2,1:T(8,128)(2,1)S(1)} %copy.93), channel_id=1, source_target_pairs={{0,1},{1,2},{2,3},{3,4},{4,5},{5,6},{6,7},{7,8},{8,9},{9,10},{10,1... | collective-permute-start | bytes 786440 | tf_op jit(solution)/shard_map/ppermute | solution.py:23
  44.5 10.0 %collective-permute-start.7 = (bf16[256,4,1,128]{3,0,2,1:T(8,128)(2,1)}, bf16[256,4,1,128]{3,0,2,1:T(8,128)(2,1)}, u32[]{:S(2)}, u32[]{:S(2)}) collective-permute-start(bf16[256,4,1,128]{3,0,2,1:T(8,128)(2,1)} %copy.96), channel_id=1, source_target_pairs={{1,0},{2,1},{3,2},{4,3},{5,4},{6,5},{7,6},{8,7},{9,8},{10,9},{11,1... | collective-permute-start | bytes 786440 | tf_op jit(solution)/shard_map/ppermute | solution.py:24
  50.3 2.3 copy-start.3
  50.3 2.3 copy-start.5
  72.3 9.1 %collective-permute-start.13 = (bf16[256,1,4,128]{0,3,2,1:T(8,128)(2,1)S(1)}, bf16[256,1,4,128]{0,3,2,1:T(8,128)(2,1)S(1)}, u32[]{:S(2)}, u32[]{:S(2)}) collective-permute-start(bf16[256,1,4,128]{0,3,2,1:T(8,128)(2,1)S(1)} %get-tuple-element.190), channel_id=1, source_target_pairs={{16,0},{0,16},{17,1},{1,17},{18,2},{2,18},{19,3},{3,19},{20,4},{4,... | collective-permute-start | bytes 786440 | tf_op jit(solution)/shard_map/ppermute | solution.py:24
  74.0 12.4 %collective-permute-start.12 = (bf16[256,1,4,128]{0,3,2,1:T(8,128)(2,1)S(1)}, bf16[256,1,4,128]{0,3,2,1:T(8,128)(2,1)S(1)}, u32[]{:S(2)}, u32[]{:S(2)}) collective-permute-start(bf16[256,1,4,128]{0,3,2,1:T(8,128)(2,1)S(1)} %get-tuple-element.189), channel_id=1, source_target_pairs={{0,16},{16,0},{1,17},{17,1},{2,18},{18,2},{3,19},{19,3},{4,20},{20... | collective-permute-start | bytes 786440 | tf_op jit(solution)/shard_map/ppermute | solution.py:23
  86.5 8.7 %collective-permute-start.14 = (bf16[256,4,1,128]{0,3,2,1:T(8,128)(2,1)S(1)}, bf16[256,4,1,128]{0,3,2,1:T(8,128)(2,1)S(1)}, u32[]{:S(2)}, u32[]{:S(2)}) collective-permute-start(bf16[256,4,1,128]{0,3,2,1:T(8,128)(2,1)S(1)} %get-tuple-element.147), channel_id=1, source_target_pairs={{0,1},{1,2},{2,3},{3,4},{4,5},{5,6},{6,7},{7,8},{8,9},{9,10},{10,1... | collective-permute-start | bytes 786440 | tf_op jit(solution)/shard_map/ppermute | solution.py:23
  86.6 8.6 %collective-permute-start.15 = (bf16[256,4,1,128]{0,3,2,1:T(8,128)(2,1)S(1)}, bf16[256,4,1,128]{0,3,2,1:T(8,128)(2,1)S(1)}, u32[]{:S(2)}, u32[]{:S(2)}) collective-permute-start(bf16[256,4,1,128]{0,3,2,1:T(8,128)(2,1)S(1)} %get-tuple-element.148), channel_id=1, source_target_pairs={{1,0},{2,1},{3,2},{4,3},{5,4},{6,5},{7,6},{8,7},{9,8},{10,9},{11,1... | collective-permute-start | bytes 786440 | tf_op jit(solution)/shard_map/ppermute | solution.py:24
  99.4 21.6 %collective-permute-start = (bf16[256,1,4,128]{0,3,2,1:T(8,128)(2,1)}, bf16[256,1,4,128]{0,3,2,1:T(8,128)(2,1)S(1)}, u32[]{:S(2)}, u32[]{:S(2)}) collective-permute-start(bf16[256,1,4,128]{0,3,2,1:T(8,128)(2,1)} %get-tuple-element.210), channel_id=1, source_target_pairs={{0,16},{16,0},{1,17},{17,1},{2,18},{18,2},{3,19},{19,3},{4,20},{20... | collective-permute-start | bytes 786440 | tf_op jit(solution)/shard_map/ppermute | solution.py:23
  101.2 19.8 %collective-permute-start.1 = (bf16[256,1,4,128]{0,3,2,1:T(8,128)(2,1)}, bf16[256,1,4,128]{0,3,2,1:T(8,128)(2,1)S(1)}, u32[]{:S(2)}, u32[]{:S(2)}) collective-permute-start(bf16[256,1,4,128]{0,3,2,1:T(8,128)(2,1)} %get-tuple-element.209), channel_id=1, source_target_pairs={{16,0},{0,16},{17,1},{1,17},{18,2},{2,18},{19,3},{3,19},{20,4},{4,... | collective-permute-start | bytes 786440 | tf_op jit(solution)/shard_map/ppermute | solution.py:24
  104.8 2.3 copy-start.104
  104.8 2.3 copy-start.106
  104.8 2.3 copy-start.108
  104.9 2.3 copy-start.110
  104.9 2.3 copy-start.112
  104.9 2.3 copy-start.114
  104.9 2.3 copy-start.116
  104.9 2.3 copy-start.118
  104.9 2.3 copy-start.120
  121.1 8.7 %collective-permute-start.3 = (bf16[256,4,1,128]{0,3,2,1:T(8,128)(2,1)S(1)}, bf16[256,4,1,128]{0,3,2,1:T(8,128)(2,1)S(1)}, u32[]{:S(2)}, u32[]{:S(2)}) collective-permute-start(bf16[256,4,1,128]{0,3,2,1:T(8,128)(2,1)S(1)} %get-tuple-element.156), channel_id=1, source_target_pairs={{0,1},{1,2},{2,3},{3,4},{4,5},{5,6},{6,7},{7,8},{8,9},{9,10},{10,1... | collective-permute-start | bytes 786440 | tf_op jit(solution)/shard_map/ppermute | solution.py:23
  121.1 8.6 %collective-permute-start.2 = (bf16[256,4,1,128]{0,3,2,1:T(8,128)(2,1)S(1)}, bf16[256,4,1,128]{0,3,2,1:T(8,128)(2,1)S(1)}, u32[]{:S(2)}, u32[]{:S(2)}) collective-permute-start(bf16[256,4,1,128]{0,3,2,1:T(8,128)(2,1)S(1)} %get-tuple-element.155), channel_id=1, source_target_pairs={{1,0},{2,1},{3,2},{4,3},{5,4},{6,5},{7,6},{8,7},{9,8},{10,9},{11,1... | collective-permute-start | bytes 786440 | tf_op jit(solution)/shard_map/ppermute | solution.py:24
  132.2 9.9 %copy-start.20 = (bf16[256,2,4,128]{0,3,2,1:T(8,128)(2,1)S(1)}, bf16[256,2,4,128]{0,3,2,1:T(8,128)(2,1)}, u32[]{:S(2)}) copy-start(bf16[256,2,4,128]{0,3,2,1:T(8,128)(2,1)} %copy-done.19) | copy-start | bytes 1572868
  152.2 134.3 %collective-permute-start.8 = (bf16[256,1,4,128]{0,3,2,1:T(8,128)(2,1)}, bf16[256,1,4,128]{0,3,2,1:T(8,128)(2,1)S(1)}, u32[]{:S(2)}, u32[]{:S(2)}) collective-permute-start(bf16[256,1,4,128]{0,3,2,1:T(8,128)(2,1)} %get-tuple-element.200), channel_id=1, source_target_pairs={{0,16},{16,0},{1,17},{17,1},{2,18},{18,2},{3,19},{19,3},{4,20},{20... | collective-permute-start | bytes 786440 | tf_op jit(solution)/shard_map/ppermute | solution.py:23
  153.9 132.5 %collective-permute-start.9 = (bf16[256,1,4,128]{0,3,2,1:T(8,128)(2,1)}, bf16[256,1,4,128]{0,3,2,1:T(8,128)(2,1)S(1)}, u32[]{:S(2)}, u32[]{:S(2)}) collective-permute-start(bf16[256,1,4,128]{0,3,2,1:T(8,128)(2,1)} %get-tuple-element.199), channel_id=1, source_target_pairs={{16,0},{0,16},{17,1},{1,17},{18,2},{2,18},{19,3},{3,19},{20,4},{4,... | collective-permute-start | bytes 786440 | tf_op jit(solution)/shard_map/ppermute | solution.py:24
  154.2 2.4 copy-start.82
  154.2 2.4 copy-start.83
  154.2 2.4 copy-start.84
  154.2 2.4 copy-start.85
  154.2 2.4 copy-start.86
  154.3 2.4 copy-start.87
  154.3 2.4 copy-start.88
  154.3 2.4 copy-start.89
  154.3 2.4 copy-start.90
  154.3 2.4 copy-start.91
  154.3 2.4 copy-start.92
  154.3 2.4 copy-start.93
  154.3 2.4 copy-start.94
  154.3 2.4 copy-start.95
  154.3 2.5 copy-start.23
  286.7 8.7 %collective-permute-start.11 = (bf16[256,4,1,128]{3,0,2,1:T(8,128)(2,1)S(1)}, bf16[256,4,1,128]{3,0,2,1:T(8,128)(2,1)S(1)}, u32[]{:S(2)}, u32[]{:S(2)}) collective-permute-start(bf16[256,4,1,128]{3,0,2,1:T(8,128)(2,1)S(1)} %copy.106), channel_id=1, source_target_pairs={{0,1},{1,2},{2,3},{3,4},{4,5},{5,6},{6,7},{7,8},{8,9},{9,10},{10,1... | collective-permute-start | bytes 786440 | tf_op jit(solution)/shard_map/ppermute | solution.py:23
  286.9 8.6 %collective-permute-start.10 = (bf16[256,4,1,128]{3,0,2,1:T(8,128)(2,1)S(1)}, bf16[256,4,1,128]{3,0,2,1:T(8,128)(2,1)S(1)}, u32[]{:S(2)}, u32[]{:S(2)}) collective-permute-start(bf16[256,4,1,128]{3,0,2,1:T(8,128)(2,1)S(1)} %copy.104), channel_id=1, source_target_pairs={{1,0},{2,1},{3,2},{4,3},{5,4},{6,5},{7,6},{8,7},{9,8},{10,9},{11,1... | collective-permute-start | bytes 786440 | tf_op jit(solution)/shard_map/ppermute | solution.py:24
  (119 other events, 207.6 us)
Sparse Core Ops, SparseCore 0:
  154.3 128.9 all-reduce.3
where the time goes:
time: 319 us; the launch traced here: 317 us
  waiting for transfers between devices  102 us (32%)
  blocking collectives  69.3 us (22%)
  other arithmetic  52 us (16%)
  local copies, waits for them, and re-layouts  31.8 us (10%)
  starting transfers between devices  27.5 us (9%)
  matrix products  17.5 us (5%)
  between operations  16.4 us (5%)
    psum x1, waiting for transfers between devices, shards(): lax.psum((partials[0], partials[1], partials[2], partials[3]), ('own', 's...  82.2 us
    psum x1, blocking collectives, shards(): lax.psum((partials[0], partials[1], partials[2], partials[3]), ('own', 's...  42.9 us
    ppermute x8, starting transfers between devices, extended(): after = lax.ppermute(first, axis, down)  23.4 us
    ppermute x8, waiting for transfers between devices, extended(): before = lax.ppermute(last, axis, up)  14.5 us
    all_gather x1, blocking collectives, shards(): lax.all_gather(dw_one, 'own', axis=1, tiled=True)  12 us
    convert_element_type x1, other arithmetic, shards(): depthwise(wide_input, taps_one, extent_x, extent_y, 1).astype(jnp.bfloat16)  11 us
    dot_general x2, matrix products, backmap(): jnp.dot(weights, flattened, preferred_element_type=jnp.float32)  10.3 us
    convert_element_type x1, other arithmetic, shards(): grad_input = (cotangent.astype(jnp.float32) + depthwise(first_padded, tap...  9.47 us
  transfers between devices with their start and end apart: 17, of which 7 were waited for; matrix products, arithmetic and copies ran while one was open for 13% of the time, Pallas kernels for 0%

commit v1 on v0

v1 whole, which is shorter than its diff:
```python
import functools
import math

import jax
import jax.numpy as jnp
from jax import lax
from jax.experimental import pallas as pl
from jax.experimental.pallas import tpu as pltpu
from jax.sharding import PartitionSpec as P

AXES = ("own", "space")
BF = jnp.bfloat16
F32 = jnp.float32
TAPS = [
    (9 * (a + 1) + 3 * (b + 1) + (d + 1), a, b, d)
    for a in (-1, 0, 1)
    for b in (-1, 0, 1)
    for d in (-1, 0, 1)
]
LANES = 128
GROUP = 16
VMEM = pl.BlockSpec(memory_space=pltpu.VMEM)
SMEM = pl.BlockSpec(memory_space=pltpu.SMEM)


def tree(terms):
    while len(terms) > 1:
        paired = [terms[i] + terms[i + 1] for i in range(0, len(terms) - 1, 2)]
        terms = paired + ([terms[-1]] if len(terms) % 2 else [])
    return terms[0]


def turned(value, shift):
    return pltpu.roll(value, shift % LANES, 1)


def conv_rows(load, weights, planes, rows, direction, emit):
    for x in range(planes):
        for y in rows:
            parts = {-1: [], 0: [], 1: []}
            for k, a, b, d in TAPS:
                parts[d].append(weights[k] * load((x + direction * a) % planes, y + direction * b))
            total = tree(parts[0]).astype(F32)
            total = total + turned(tree(parts[1]).astype(F32), -direction)
            total = total + turned(tree(parts[-1]).astype(F32), direction)
            emit(x, y, total)


def tap_products(load, gradient, planes, rows, emit):
    turns = {}
    for x in range(planes):
        for y in rows:
            value = gradient(x, y)
            wide = value.astype(F32)
            turns[x, y] = {-1: turned(wide, -1).astype(BF), 0: value, 1: turned(wide, 1).astype(BF)}
    for k, a, b, d in TAPS:
        emit(k, tree([load((x + a) % planes, y + b) * turns[x, y][d] for x in range(planes) for y in rows]))


def side_by_side(slabs):
    return jnp.concatenate(slabs, axis=1)


def channel_groups(body, channels):
    def step(group, carry):
        body(pl.ds(pl.multiple_of(group * GROUP, GROUP), GROUP))
        return carry

    lax.fori_loop(0, channels // GROUP, step, 0)


def contract(left, right):
    return lax.dot_general(left, right, (((1,), (1,)), ((), ())), preferred_element_type=F32)


def fill_extended(own, ext, local, beside, strip, rest, halo, halo_beside, height):
    del strip
    span = height + 2
    for x in range(2):
        for y in range(height):
            ext[x * span + 2 * (1 - own) + y] = local[x * height + y]
        for y in range(2):
            ext[x * span + 4 * own + y] = halo[x * 2 + y]
            ext[(x + 2) * span + 4 * own + y] = halo_beside[x * 2 + y]
            ext[(x + 2) * span + 2 + y] = beside[x * 2 + y]
            ext[(x + 2) * span + 4 * (1 - own) + y] = rest[x * 2 + y]


def forward_kernel(own_ref, local, beside, rest, halo, halo_beside, taps, weight_t, ext, first, act, slope):
    own = own_ref[0]
    channels = local.shape[1]
    fill_extended(own, ext, local, beside, None, rest, halo, halo_beside, 4)

    def group(rows):
        weights = [taps[k, rows, :] for k in range(27)]

        def emit(x, y, total):
            first[x * 4 + y - 1, rows, :] = total.astype(BF)

        conv_rows(lambda x, y: ext[x * 6 + y, rows, :], weights, 4, range(1, 5), 1, emit)

    channel_groups(group, channels)

    def pointwise(step, carry):
        base = step * 4
        source = side_by_side([first[base + j] for j in range(4)])
        pre = jnp.dot(weight_t[...], source, preferred_element_type=F32)
        sigma = jax.nn.sigmoid(pre)
        value = (pre * sigma).astype(BF)
        factor = (sigma * (1.0 + pre * (1.0 - sigma))).astype(BF)
        for j in range(4):
            act[base + j] = value[:, j * LANES : (j + 1) * LANES]
            slope[base + j] = factor[:, j * LANES : (j + 1) * LANES]
        return carry

    lax.fori_loop(0, 4, pointwise, 0)


def second_kernel(own_ref, act, local, beside, taps, weight, selector, grad_pw, grad_dw, second, grad_second, cotan, products):
    own = own_ref[0]
    channels = act.shape[1]
    for x in range(2):
        for y in range(2):
            cotan[x * 2 + y] = local[x * 4 + 2 * own + y]
            cotan[(x + 2) * 2 + y] = beside[x * 2 + y]
    for x in range(4):
        source = side_by_side([cotan[x * 2], cotan[x * 2 + 1]])
        value = jnp.dot(weight[...], source, preferred_element_type=F32).astype(BF)
        grad_second[x * 2] = value[:, :LANES]
        grad_second[x * 2 + 1] = value[:, LANES:]

    def group(rows):
        weights = [taps[k, rows, :] for k in range(27)]
        load = lambda x, y: act[x * 4 + y, rows, :]

        def emit(x, y, total):
            second[x * 2 + y - 1, rows, :] = total.astype(BF)

        conv_rows(load, weights, 4, range(1, 3), 1, emit)

        def keep(k, value):
            products[rows, k * LANES : (k + 1) * LANES] = value

        tap_products(load, lambda x, y: grad_second[x * 2 + y - 1, rows, :], 4, range(1, 3), keep)

    channel_groups(group, channels)
    total = jnp.zeros((channels, channels), F32)
    for x in range(4):
        total += contract(side_by_side([second[2 * x], second[2 * x + 1]]), side_by_side([cotan[2 * x], cotan[2 * x + 1]]))
    grad_pw[...] = total
    grad_dw[...] = jnp.dot(products[...], selector[...], preferred_element_type=F32)


def backward_kernel(
    own_ref, local, beside, rest, halo, halo_beside, slope, first, density, taps, weight_two, weight_one, selector,
    grad_first, grad_pw, grad_dw, ext, grad_second, grad_pre, products,
):
    own = own_ref[0]
    channels = local.shape[1]
    fill_extended(own, ext, local, beside, None, rest, halo, halo_beside, 4)

    def pointwise(step, carry):
        source = side_by_side([ext[step * 4 + j] for j in range(4)])
        value = jnp.dot(weight_two[...], source, preferred_element_type=F32).astype(BF)
        for j in range(4):
            grad_second[step * 4 + j] = value[:, j * LANES : (j + 1) * LANES]
        return carry

    lax.fori_loop(0, 6, pointwise, 0)

    def group(rows):
        weights = [taps[k, rows, :] for k in range(27)]

        def emit(x, y, total):
            slab = x * 4 + y - 1
            grad_pre[slab, rows, :] = (total * slope[slab, rows, :].astype(F32)).astype(BF)

        conv_rows(lambda x, y: grad_second[x * 6 + y, rows, :], weights, 4, range(1, 5), -1, emit)

    channel_groups(group, channels)

    def backmap(step, carry):
        source = side_by_side([grad_pre[step * 4 + j] for j in range(4)])
        value = jnp.dot(weight_one[...], source, preferred_element_type=F32).astype(BF)
        for j in range(4):
            grad_first[step * 4 + j] = value[:, j * LANES : (j + 1) * LANES]
        return carry

    lax.fori_loop(0, 4, backmap, 0)
    total = jnp.zeros((channels, channels), F32)
    for x in range(4):
        total += contract(
            side_by_side([first[4 * x + 1], first[4 * x + 2]]), side_by_side([grad_pre[4 * x + 1], grad_pre[4 * x + 2]])
        )
    grad_pw[...] = total

    def tap_group(rows):
        def keep(k, value):
            products[rows, k * LANES : (k + 1) * LANES] = value

        tap_products(
            lambda x, y: density[x * 6 + y, rows, :], lambda x, y: grad_first[x * 4 + y - 1, rows, :], 4, range(2, 4), keep
        )

    channel_groups(tap_group, channels)
    grad_dw[...] = jnp.dot(products[...], selector[...], preferred_element_type=F32)


def input_kernel(own_ref, local, beside, grad_first, taps, mine, other):
    own = own_ref[0]
    channels = local.shape[1]

    def group(rows):
        weights = [taps[k, rows, :] for k in range(27)]

        def emit(x, y, total):
            slab = (x % 2) * 2 + y - 1
            if x < 2:
                mine[slab, rows, :] = (local[x * 4 + 2 * own + y - 1, rows, :].astype(F32) + total).astype(BF)
            else:
                other[slab, rows, :] = (beside[slab, rows, :].astype(F32) + total).astype(BF)

        conv_rows(lambda x, y: grad_first[x * 4 + y, rows, :], weights, 4, range(1, 3), -1, emit)

    channel_groups(group, channels)


def call(kernel, name, outs, scratch, inputs, flops):
    return pl.pallas_call(
        kernel,
        name=name,
        out_shape=[jax.ShapeDtypeStruct(shape, dtype) for shape, dtype in outs],
        in_specs=[SMEM] + [VMEM] * (len(inputs) - 1),
        out_specs=[VMEM] * len(outs),
        scratch_shapes=[pltpu.VMEM(shape, dtype) for shape, dtype in scratch],
        compiler_params=pltpu.CompilerParams(vmem_limit_bytes=48 * 1024 * 1024),
        cost_estimate=pl.CostEstimate(flops=flops, bytes_accessed=4 * 1024 * 1024, transcendentals=0),
    )(*inputs)


def shards(density, cotangent, pw_one, pw_two, dw_one, dw_two):
    channels, extent_x, extent_y, extent_z = density.shape
    own_size, space_size = lax.axis_size("own"), lax.axis_size("space")
    own = lax.axis_index("own")
    place = lambda o, s: o * space_size + s % space_size
    every = [(o, s) for o in range(own_size) for s in range(space_size)]
    across = [(place(o, s), place(1 - o, s)) for o, s in every]
    onward = [(place(o, s), place(o, s + 1 - 2 * o)) for o, s in every]
    swap = lambda value: lax.ppermute(value, AXES, across)
    pass_on = lambda value: lax.ppermute(value, AXES, onward)
    slabs = 2 * extent_x
    own_ref = own.astype(jnp.int32).reshape(1)

    def gathered(value, axis):
        other = swap(value)
        return jnp.where(own == 0, jnp.concatenate([value, other], axis), jnp.concatenate([other, value], axis))

    def pieces(value):
        rows = value.transpose(1, 2, 0, 3)
        strip = lax.dynamic_slice_in_dim(rows, 2 * own, 2, 1).reshape(slabs, channels, extent_z)
        rest = lax.dynamic_slice_in_dim(rows, 2 - 2 * own, 2, 1).reshape(slabs, channels, extent_z)
        return rows.reshape(extent_x * extent_y, channels, extent_z), strip, rest

    dw_both = gathered(jnp.concatenate([dw_one, dw_two], 0), 1)
    density_rows, density_strip, density_rest = pieces(density)
    density_far = swap(density_strip)
    density_beside = swap(density_rest)
    density_halo = pass_on(density_rest)
    density_halo_far = pass_on(density_far)
    pw_both = gathered(jnp.stack([pw_one, pw_two]), 1)
    cot_rows, cot_strip, cot_rest = pieces(cotangent)
    cot_far = swap(cot_strip)
    cot_beside = swap(cot_rest)
    cot_halo = pass_on(cot_rest)
    cot_halo_far = pass_on(cot_far)

    taps_one = jnp.broadcast_to(dw_both[:27, :, None], (27, channels, LANES))
    taps_two = jnp.broadcast_to(dw_both[27:, :, None], (27, channels, LANES))
    weight_one, weight_two = pw_both[0], pw_both[1]
    selector = (lax.broadcasted_iota(jnp.int32, (27 * LANES, LANES), 0) // LANES == lax.broadcasted_iota(jnp.int32, (27 * LANES, LANES), 1)).astype(BF)

    slab = (channels, LANES)
    density_ext, first, act, slope = call(
        forward_kernel, "forward",
        [((24,) + slab, BF), ((16,) + slab, BF), ((16,) + slab, BF), ((16,) + slab, BF)], [],
        (own_ref, density_rows, density_beside, density_far, density_halo, density_halo_far, taps_one, weight_one.T),
        5_000_000_000,
    )
    pw_two_part, dw_two_part = call(
        second_kernel, "second",
        [((channels, channels), F32), ((channels, LANES), F32)],
        [((8,) + slab, BF), ((8,) + slab, BF), ((8,) + slab, BF), ((channels, 27 * LANES), BF)],
        (own_ref, act, cot_rows, cot_beside, taps_two, weight_two, selector),
        5_000_000_000,
    )
    grad_first, pw_one_part, dw_one_part = call(
        backward_kernel, "backward",
        [((16,) + slab, BF), ((channels, channels), F32), ((channels, LANES), F32)],
        [((24,) + slab, BF), ((24,) + slab, BF), ((16,) + slab, BF), ((channels, 27 * LANES), BF)],
        (own_ref, cot_rows, cot_beside, cot_far, cot_halo, cot_halo_far, slope, first, density_ext, taps_two, weight_two, weight_one, selector),
        5_000_000_000,
    )
    mine, other = call(
        input_kernel, "input",
        [((4,) + slab, BF), ((4,) + slab, BF)], [],
        (own_ref, cot_rows, cot_beside, grad_first, taps_one),
        3_000_000_000,
    )

    def summed(pw_part, dw_part):
        half = channels // 2
        both = jnp.concatenate([pw_part, dw_part], 1).astype(BF)
        keep = lax.dynamic_slice_in_dim(both, own * half, half, 0)
        give = lax.dynamic_slice_in_dim(both, half - own * half, half, 0)
        total = keep.astype(F32) + swap(give).astype(F32)
        step = 1
        while step < space_size:
            pairs = [(place(o, s), place(o, s ^ step)) for o, s in every]
            sent = total.astype(BF)
            total = sent.astype(F32) + lax.ppermute(sent, AXES, pairs).astype(F32)
            step *= 2
        total = total * (1.0 / math.sqrt(float(extent_x * extent_y * extent_z * own_size * space_size)))
        return total[:, :channels], total[:, channels : channels + 27].T

    grad_pw_two, grad_dw_two = summed(pw_two_part, dw_two_part)
    grad_pw_one, grad_dw_one = summed(pw_one_part, dw_one_part)
    back = swap(other)
    mine = mine.reshape(2, 2, channels, extent_z)
    back = back.reshape(2, 2, channels, extent_z)
    rows = jnp.where(own == 0, jnp.concatenate([mine, back], 1), jnp.concatenate([back, mine], 1))
    grad_input = rows.transpose(2, 0, 1, 3)
    return grad_input, grad_pw_one, grad_pw_two, grad_dw_one, grad_dw_two


def solution(mesh):
    in_specs = (
        P(None, "own", "space", None),
        P(None, "own", "space", None),
        P("own", None),
        P("own", None),
        P(None, "own"),
        P(None, "own"),
    )
    out_specs = (
        P(None, "own", "space", None),
        P("own", None),
        P("own", None),
        P(None, "own"),
        P(None, "own"),
    )
    return jax.shard_map(shards, mesh=mesh, in_specs=in_specs, out_specs=out_specs, check_vma=False)
```

time: 319 us -> 102 us (0.32)
  waiting for transfers between devices: 102 us -> 21.7 us
  blocking collectives: 69.3 us -> 0 us
  other arithmetic: 52 us -> 6.93 us
  Pallas kernels: 0 us -> 29.8 us
  local copies, waits for them, and re-layouts: 31.8 us -> 13.9 us
  matrix products: 17.5 us -> 0 us
  between operations: 16.4 us -> 0.98 us
    psum x1 -> x0, waiting for transfers between devices: 82.2 us -> none  [shards(): lax.psum((partials[0], partials[1], partials[2], partials[3]), ('own', 's...]
    psum x1 -> x0, blocking collectives: 42.9 us -> none  [shards(): lax.psum((partials[0], partials[1], partials[2], partials[3]), ('own', 's...]
    convert_element_type x10 -> x9, other arithmetic: 36.3 us -> 3.2 us  [the longest x1 2.97 us: shards(): (lax.broadcasted_iota(jnp.int32, (27 * LANES, LANES), 0) // LANES == lax....]
    pallas_call x0 -> x4, Pallas kernels: none -> 29.8 us  [call(): pl.pallas_call(kernel, name=name, out_shape=[jax.ShapeDtypeStruct(shape,...]
    all_gather x4 -> x0, blocking collectives: 26.3 us -> none  [the longest x1 12 us: shards(): lax.all_gather(dw_one, 'own', axis=1, tiled=True)]
    dot_general x5 -> x0, matrix products: 17.5 us -> none  [the longest x2 10.3 us: backmap(): jnp.dot(weights, flattened, preferred_element_type=jnp.float32)]
    reduce_sum x5 -> x0, other arithmetic: 8.24 us -> none  [tap_sums(): columns.append(jnp.sum(shifted * grad_float, axis=(1, 2, 3)))]
    slice x17 -> x3, local copies, waits for them, and re-layouts: 9.01 us -> 1.34 us  [the longest x2 1.33 us: summed(): return (total[:, :channels], total[:, channels:channels + 27].T)]
  transfers between devices with their start and end apart: 17 -> 21, of which waited for: 7 -> 8; matrix products, arithmetic and copies ran while one was open for 13% -> 14% of each run, Pallas kernels for 0% -> 29%
where the time goes in v1:
time: 102 us; the launch traced here: 101 us
  Pallas kernels  29.8 us (29%)
  starting transfers between devices  28.1 us (28%)
  waiting for transfers between devices  21.7 us (21%)
  local copies, waits for them, and re-layouts  13.9 us (14%)
  other arithmetic  6.93 us (7%)
    pallas_call x4, Pallas kernels, call(): pl.pallas_call(kernel, name=name, out_shape=[jax.ShapeDtypeStruct(shape,...  29.8 us
    ppermute x9, starting transfers between devices, shards(): swap = lambda value: lax.ppermute(value, AXES, across)  17.2 us
    ppermute x9, waiting for transfers between devices, shards(): swap = lambda value: lax.ppermute(value, AXES, across)  11.8 us
    ppermute x8, waiting for transfers between devices, summed(): total = sent.astype(F32) + lax.ppermute(sent, AXES, pairs).astype(F32)  9.92 us
    ppermute x8, starting transfers between devices, summed(): total = sent.astype(F32) + lax.ppermute(sent, AXES, pairs).astype(F32)  9.01 us
    dynamic_slice x3, local copies, waits for them, and re-layouts, pieces(): lax.dynamic_slice_in_dim(rows, 2 * own, 2, 1)  4.84 us
    convert_element_type x1, other arithmetic, shards(): (lax.broadcasted_iota(jnp.int32, (27 * LANES, LANES), 0) // LANES == lax....  2.97 us
    dynamic_slice x2, local copies, waits for them, and re-layouts, pieces(): lax.dynamic_slice_in_dim(rows, 2 - 2 * own, 2, 1)  2.42 us
  transfers between devices with their start and end apart: 21, of which 8 were waited for; matrix products, arithmetic and copies ran while one was open for 14% of the time, Pallas kernels for 29%

profile of v1, /device:TPU:0, one launch (start us, length us, event | category | flops | bytes accessed | tf_op | source)
XLA Modules:
  0.0 101.4 jit_solution(5899250629259211875)
XLA Ops:
  0.7 3.4 %dynamic-slice_bitcast_fusion = (bf16[2,2,256,128]{3,1,0,2:T(2,128)(2,1)S(1)}, bf16[2,2,256,128]{3,1,0,2:T(2,128)(2,1)S(1)}, bf16[2,2,256,128]{3,1,0,2:T(2,128)(2,1)}, bf16[2,2,256,128]{3,1,0,2:T(2,128)(2,1)S(1)}) fusion(bf16[256,2,4,128]{3,2,1,0:T(4,128)(2,1)} %param.6, s32[]{:T(128)S(6)} %select_n.49, s32[]{:T(128)S(6)} %select_n.48, ...), kind=kLoop, calls=%fused_computation.5 | loop fusion | bytes 2097160 | tf_op jit(solution)/shard_map/dynamic_slice | solution.py:260
  4.1 0.7 copy.15
  4.8 3.0 %collective-permute-start.4 = (bf16[4,256,128]{2,1,0:T(8,128)(2,1)}, bf16[4,256,128]{2,1,0:T(8,128)(2,1)S(1)}, u32[]{:S(2)}, u32[]{:S(2)}) collective-permute-start(bf16[4,256,128]{2,1,0:T(8,128)(2,1)} %bitcast.10), channel_id=1, source_target_pairs={{0,16},{1,17},{2,18},{3,19},{4,20},{5,21},{6,22},{7,23},{8,24},{9,... | collective-permute-start | bytes 786440 | tf_op jit(solution)/shard_map/ppermute | solution.py:249
  7.8 0.7 copy.16
  8.5 4.2 %collective-permute-start.5 = (bf16[4,256,128]{2,1,0:T(8,128)(2,1)}, bf16[4,256,128]{2,1,0:T(8,128)(2,1)S(1)}, u32[]{:S(2)}, u32[]{:S(2)}) collective-permute-start(bf16[4,256,128]{2,1,0:T(8,128)(2,1)} %bitcast.12), channel_id=1, source_target_pairs={{0,16},{1,17},{2,18},{3,19},{4,20},{5,21},{6,22},{7,23},{8,24},{9,... | collective-permute-start | bytes 786440 | tf_op jit(solution)/shard_map/ppermute | solution.py:249
  12.7 0.7 pad_maximum_fusion
  13.4 2.1 %collective-permute-start.8 = (bf16[54,128]{1,0:T(8,128)(2,1)S(1)}, bf16[54,128]{1,0:T(8,128)(2,1)S(1)}, u32[]{:S(2)}, u32[]{:S(2)}) collective-permute-start(bf16[54,128]{1,0:T(8,128)(2,1)S(1)} %pad_maximum_fusion.1), channel_id=1, source_target_pairs={{0,16},{1,17},{2,18},{3,19},{4,20},{5,21},{6,22},{7,23},{8,24},{9,... | collective-permute-start | bytes 41480 | tf_op jit(solution)/shard_map/ppermute | solution.py:249
  15.5 3.0 %fusion.selector = bf16[3456,128]{1,0:T(8,128)(2,1)S(1)} fusion(s32[3456]{0:T(1024)S(1)} %get-tuple-element.43, s32[3456]{0:T(1024)S(1)} %get-tuple-element.44, pred[3456]{0:T(1024)(128)(4,1)S(1)} %fusion.8), kind=kLoop, calls=%fused_computation.1 | loop fusion | flops 1327104 | bytes 915840 | tf_op jit(solution)/shard_map/convert_element_type | solution.py:280
  18.5 0.1 copy.14
  18.6 1.7 %copy.12 = bf16[2,2,256,128]{3,2,1,0:T(8,128)(2,1)} copy(bf16[2,2,256,128]{3,1,0,2:T(2,128)(2,1)} %get-tuple-element.41) | data formatting | bytes 524288 | tf_op jit(solution)/shard_map/dynamic_slice | solution.py:261
  20.3 0.7 copy.13
  21.1 1.9 %collective-permute-done.8 = bf16[54,128]{1,0:T(8,128)(2,1)S(1)} collective-permute-done((bf16[54,128]{1,0:T(8,128)(2,1)S(1)}, bf16[54,128]{1,0:T(8,128)(2,1)S(1)}, u32[]{:S(2)}, u32[]{:S(2)}) %collective-permute-start.8) | collective-permute-done | bytes 13856 | tf_op jit(solution)/shard_map/ppermute | solution.py:249
  23.0 1.7 %collective-permute-start = (bf16[4,256,128]{2,1,0:T(8,128)(2,1)}, bf16[4,256,128]{2,1,0:T(8,128)(2,1)S(1)}, u32[]{:S(2)}, u32[]{:S(2)}) collective-permute-start(bf16[4,256,128]{2,1,0:T(8,128)(2,1)} %bitcast.41), channel_id=1, source_target_pairs={{0,16},{1,17},{2,18},{3,19},{4,20},{5,21},{6,22},{7,23},{8,24},{9,... | collective-permute-start | bytes 786440 | tf_op jit(solution)/shard_map/ppermute | solution.py:249
  24.8 0.3 collective-permute-start.1
  25.1 1.1 %maximum_select_fusion.1 = bf16[2,256,256]{2,1,0:T(8,128)(2,1)S(1)} fusion(bf16[2,128,256]{2,1,0:T(8,128)(2,1)} %collective-permute-done.9, bf16[1,128,256]{2,1,0:T(8,128)(2,1)} %bitcast.44, bf16[1,128,256]{2,1,0:T(8,128)(2,1)} %bitcast.46, pred[]{:T(512)S(6)} %eq.10), kind=kLoop, calls=%fused_computation.4 | loop fusion | flops 1703936 | bytes 524289 | tf_op jit(solution)/shard_map/jit(_where)/select_n | solution.py:256
  26.3 0.1 copy.17.weight_t
  26.4 1.9 %collective-permute-start.2 = (bf16[4,256,128]{2,1,0:T(8,128)(2,1)}, bf16[4,256,128]{2,1,0:T(8,128)(2,1)S(1)}, u32[]{:S(2)}, u32[]{:S(2)}) collective-permute-start(bf16[4,256,128]{2,1,0:T(8,128)(2,1)} %bitcast.42), channel_id=1, source_target_pairs={{0,1},{1,2},{2,3},{3,4},{4,5},{5,6},{6,7},{7,8},{8,9},{9,10},{10,1... | collective-permute-start | bytes 786440 | tf_op jit(solution)/shard_map/ppermute | solution.py:250
  28.3 8.2 %collective-permute-done.1.rest = bf16[4,256,128]{2,1,0:T(8,128)(2,1)} collective-permute-done((bf16[4,256,128]{2,1,0:T(8,128)(2,1)}, bf16[4,256,128]{2,1,0:T(8,128)(2,1)}, u32[]{:S(2)}, u32[]{:S(2)}) %collective-permute-start.1) | collective-permute-done | bytes 262176 | tf_op jit(solution)/shard_map/ppermute | solution.py:249
  36.5 2.0 %broadcast_in_dim.4.taps = bf16[27,256,128]{2,1,0:T(8,128)(2,1)} broadcast(bf16[27,256]{1,0:T(8,128)(2,1)S(1)} %get-tuple-element.40), dimensions={0,1} | broadcast | bytes 1783296 | tf_op jit(solution)/shard_map/broadcast_in_dim | solution.py:277
  38.5 8.2 %forward.1 = (bf16[24,256,128]{2,1,0:T(8,128)(2,1)}, bf16[16,256,128]{2,1,0:T(8,128)(2,1)S(1)}, bf16[16,256,128]{2,1,0:T(8,128)(2,1)S(1)}, bf16[16,256,128]{2,1,0:T(8,128)(2,1)S(1)}) custom-call(s32[1]{0:T(128)} %bitcast.own_ref, bf16[8,256,128]{2,1,0:T(8,128)(2,1)S(1)} %bitcast.37, bf16[4,256,128]{2,1,0:T(8,128)(2,1)S(1)} %collective-permute-done.4.beside, ...), custom_call_target="tpu_custom_call" | custom-call | flops 5000000000 | bytes 4194304 | tf_op jit(solution)/shard_map/forward/pallas_call | solution.py:229
  46.8 1.1 %broadcast_in_dim.5.taps = bf16[27,256,128]{2,1,0:T(8,128)(2,1)S(1)} broadcast(bf16[27,256]{1,0:T(8,128)(2,1)S(1)} %get-tuple-element.39), dimensions={0,1} | broadcast | bytes 1783296 | tf_op jit(solution)/shard_map/broadcast_in_dim | solution.py:278
  47.9 5.7 %second.1 = (f32[256,256]{1,0:T(8,128)S(1)}, f32[256,128]{1,0:T(8,128)S(1)}) custom-call(s32[1]{0:T(128)} %bitcast.own_ref, bf16[16,256,128]{2,1,0:T(8,128)(2,1)S(1)} %get-tuple-element.24.act, bf16[8,256,128]{2,1,0:T(8,128)(2,1)S(1)} %bitcast.34, bf16[4,256,128]{2,1,0:T(8,128)(2,1)S(1)} %collective-permute-done.beside, ...), custom_call_target="tpu_custom_call" | custom-call | flops 5000000000 | bytes 4194304 | tf_op jit(solution)/shard_map/second/pallas_call | solution.py:229
  53.7 3.7 %collective-permute-start.16 = (bf16[128,384]{1,0:T(8,128)(2,1)S(1)}, bf16[128,384]{1,0:T(8,128)(2,1)S(1)}, u32[]{:S(2)}, u32[]{:S(2)}) collective-permute-start(bf16[128,384]{1,0:T(8,128)(2,1)S(1)} %fusion.2), channel_id=1, source_target_pairs={{0,16},{1,17},{2,18},{3,19},{4,20},{5,21},{6,22},{7,23},{8,24},{9,... | collective-permute-start | bytes 294920 | tf_op jit(solution)/shard_map/ppermute | solution.py:249
  57.4 13.2 %backward.1 = (bf16[16,256,128]{2,1,0:T(8,128)(2,1)S(1)}, f32[256,256]{1,0:T(8,128)S(1)}, f32[256,128]{1,0:T(8,128)S(1)}) custom-call(s32[1]{0:T(128)} %bitcast.own_ref, bf16[8,256,128]{2,1,0:T(8,128)(2,1)S(1)} %bitcast.35, bf16[4,256,128]{2,1,0:T(8,128)(2,1)S(1)} %collective-permute-done.beside, bf16[4,256,128]{2,1,0:T(8,128)(2,1)} %collective-permute-done.1.rest, ...), custom_call_target="tpu_custom_call" | custom-call | flops 5000000000 | bytes 4194304 | tf_op jit(solution)/shard_map/backward/pallas_call | solution.py:229
  70.7 0.1 collective-permute-start.11
  70.8 2.6 %input.1 = (bf16[4,256,128]{2,1,0:T(8,128)(2,1)S(1)}, bf16[4,256,128]{2,1,0:T(8,128)(2,1)S(1)}) custom-call(s32[1]{0:T(128)} %bitcast.own_ref, bf16[8,256,128]{2,1,0:T(8,128)(2,1)S(1)} %bitcast.36, bf16[4,256,128]{2,1,0:T(8,128)(2,1)S(1)} %collective-permute-done.beside, bf16[16,256,128]{2,1,0:T(8,128)(2,1)S(1)} %get-tuple-element.19.grad_first, ...), custom_call_target="tpu_custom_call" | custom-call | flops 3000000000 | bytes 4194304 | tf_op jit(solution)/shard_map/input/pallas_call | solution.py:229
  73.4 2.1 %collective-permute-start.10 = (bf16[4,256,128]{2,1,0:T(8,128)(2,1)S(1)}, bf16[4,256,128]{2,1,0:T(8,128)(2,1)S(1)}, u32[]{:S(2)}, u32[]{:S(2)}) collective-permute-start(bf16[4,256,128]{2,1,0:T(8,128)(2,1)S(1)} %get-tuple-element.21), channel_id=1, source_target_pairs={{0,16},{1,17},{2,18},{3,19},{4,20},{5,21},{6,22},{7,23},{8,24},{9,... | collective-permute-start | bytes 786440 | tf_op jit(solution)/shard_map/ppermute | solution.py:249
  75.5 0.3 copy.18
  75.8 0.1 collective-permute-start.17
  76.0 0.5 collective-permute-start.12
  76.5 0.7 collective-permute-done.17
  77.2 0.1 collective-permute-start.18
  77.3 0.1 collective-permute-done.12
  77.5 1.9 %collective-permute-start.13 = (bf16[128,384]{1,0:T(8,128)(2,1)S(1)}, bf16[128,384]{1,0:T(8,128)(2,1)S(1)}, u32[]{:S(2)}, u32[]{:S(2)}) collective-permute-start(bf16[128,384]{1,0:T(8,128)(2,1)S(1)} %add_convert_fusion.6), channel_id=1, source_target_pairs={{0,2},{1,3},{2,0},{3,1},{4,6},{5,7},{6,4},{7,5},{8,10},{9,11},{10,... | collective-permute-start | bytes 294920 | tf_op jit(solution)/shard_map/ppermute | solution.py:320
  79.4 1.6 %collective-permute-done.10 = bf16[4,256,128]{2,1,0:T(8,128)(2,1)S(1)} collective-permute-done((bf16[4,256,128]{2,1,0:T(8,128)(2,1)S(1)}, bf16[4,256,128]{2,1,0:T(8,128)(2,1)S(1)}, u32[]{:S(2)}, u32[]{:S(2)}) %collective-permute-start.10) | collective-permute-done | bytes 262176 | tf_op jit(solution)/shard_map/ppermute | solution.py:249
  81.0 0.3 copy.19
  81.3 1.7 %fusion.1 = bf16[256,2,4,128]{3,2,1,0:T(4,128)(2,1)} fusion(bf16[2,2,256,128]{3,1,0,2:T(2,128)(2,1)S(1)} %copy.19, bf16[2,2,256,128]{3,1,0,2:T(2,128)(2,1)S(1)} %copy.18, pred[]{:T(512)S(6)} %eq.10), kind=kLoop, calls=%fused_computation.3 | loop fusion | flops 2359296 | bytes 1048577 | tf_op jit(solution)/shard_map/transpose | solution.py:331
  83.1 1.5 %collective-permute-start.19 = (bf16[128,384]{1,0:T(8,128)(2,1)S(1)}, bf16[128,384]{1,0:T(8,128)(2,1)S(1)}, u32[]{:S(2)}, u32[]{:S(2)}) collective-permute-start(bf16[128,384]{1,0:T(8,128)(2,1)S(1)} %add_convert_fusion.1), channel_id=1, source_target_pairs={{0,4},{1,5},{2,6},{3,7},{4,0},{5,1},{6,2},{7,3},{8,12},{9,13},{10,... | collective-permute-start | bytes 294920 | tf_op jit(solution)/shard_map/ppermute | solution.py:320
  84.6 0.7 collective-permute-start.14
  85.3 3.2 %collective-permute-done.19 = bf16[128,384]{1,0:T(8,128)(2,1)S(1)} collective-permute-done((bf16[128,384]{1,0:T(8,128)(2,1)S(1)}, bf16[128,384]{1,0:T(8,128)(2,1)S(1)}, u32[]{:S(2)}, u32[]{:S(2)}) %collective-permute-start.19) | collective-permute-done | bytes 98336 | tf_op jit(solution)/shard_map/ppermute | solution.py:320
  88.5 2.8 %collective-permute-start.20 = (bf16[128,384]{1,0:T(8,128)(2,1)S(1)}, bf16[128,384]{1,0:T(8,128)(2,1)S(1)}, u32[]{:S(2)}, u32[]{:S(2)}) collective-permute-start(bf16[128,384]{1,0:T(8,128)(2,1)S(1)} %add_convert_fusion), channel_id=1, source_target_pairs={{0,8},{1,9},{2,10},{3,11},{4,12},{5,13},{6,14},{7,15},{8,0},{9,1},... | collective-permute-start | bytes 294920 | tf_op jit(solution)/shard_map/ppermute | solution.py:320
  91.3 1.5 %collective-permute-start.15 = (bf16[128,384]{1,0:T(8,128)(2,1)S(1)}, bf16[128,384]{1,0:T(8,128)(2,1)S(1)}, u32[]{:S(2)}, u32[]{:S(2)}) collective-permute-start(bf16[128,384]{1,0:T(8,128)(2,1)S(1)} %add_convert_fusion.4), channel_id=1, source_target_pairs={{0,8},{1,9},{2,10},{3,11},{4,12},{5,13},{6,14},{7,15},{8,0},{9,1},... | collective-permute-start | bytes 294920 | tf_op jit(solution)/shard_map/ppermute | solution.py:320
  92.8 5.4 %collective-permute-done.20 = bf16[128,384]{1,0:T(8,128)(2,1)S(1)} collective-permute-done((bf16[128,384]{1,0:T(8,128)(2,1)S(1)}, bf16[128,384]{1,0:T(8,128)(2,1)S(1)}, u32[]{:S(2)}, u32[]{:S(2)}) %collective-permute-start.20) | collective-permute-done | bytes 98336 | tf_op jit(solution)/shard_map/ppermute | solution.py:320
  98.2 0.7 slice.37
  98.9 0.5 collective-permute-done.15
  99.4 0.7 slice.36
  100.1 0.7 copy.23
  100.7 0.7 copy.22
  (60 shorter events, 0.6 us)
Async XLA Ops:
  0.6 12.1 %copy-start.6 = (bf16[128,256]{1,0:T(8,128)(2,1)S(1)}, bf16[128,256]{1,0:T(8,128)(2,1)}, u32[]{:S(2)}) copy-start(bf16[128,256]{1,0:T(8,128)(2,1)} %param.8) | copy-start | bytes 196612
  0.6 12.0 %copy-start.5 = (bf16[128,256]{1,0:T(8,128)(2,1)S(1)}, bf16[128,256]{1,0:T(8,128)(2,1)}, u32[]{:S(2)}) copy-start(bf16[128,256]{1,0:T(8,128)(2,1)} %param.9) | copy-start | bytes 196612
  0.7 12.7 %copy-start.8 = (bf16[27,128]{1,0:T(8,128)(2,1)S(1)}, bf16[27,128]{1,0:T(8,128)(2,1)}, u32[]{:S(2)}) copy-start(bf16[27,128]{1,0:T(8,128)(2,1)} %param.10) | copy-start | bytes 20740
  0.7 12.7 %copy-start.7 = (bf16[27,128]{1,0:T(8,128)(2,1)S(1)}, bf16[27,128]{1,0:T(8,128)(2,1)}, u32[]{:S(2)}) copy-start(bf16[27,128]{1,0:T(8,128)(2,1)} %param.11) | copy-start | bytes 20740
  0.7 17.8 %copy-start.3 = (bf16[256,2,4,128]{3,2,1,0:T(4,128)(2,1)S(1)}, bf16[256,2,4,128]{3,2,1,0:T(4,128)(2,1)}, u32[]{:S(2)}) copy-start(bf16[256,2,4,128]{3,2,1,0:T(4,128)(2,1)} %param.6) | copy-start | bytes 1572868
  4.8 15.5 %copy-start.4 = (bf16[256,2,4,128]{3,2,1,0:T(4,128)(2,1)S(1)}, bf16[256,2,4,128]{3,2,1,0:T(4,128)(2,1)}, u32[]{:S(2)}) copy-start(bf16[256,2,4,128]{3,2,1,0:T(4,128)(2,1)} %param.7) | copy-start | bytes 1572868
  4.8 21.6 %collective-permute-start.4 = (bf16[4,256,128]{2,1,0:T(8,128)(2,1)}, bf16[4,256,128]{2,1,0:T(8,128)(2,1)S(1)}, u32[]{:S(2)}, u32[]{:S(2)}) collective-permute-start(bf16[4,256,128]{2,1,0:T(8,128)(2,1)} %bitcast.10), channel_id=1, source_target_pairs={{0,16},{1,17},{2,18},{3,19},{4,20},{5,21},{6,22},{7,23},{8,24},{9,... | collective-permute-start | bytes 786440 | tf_op jit(solution)/shard_map/ppermute | solution.py:249
  7.8 28.8 %collective-permute-start.6 = (bf16[4,256,128]{2,1,0:T(8,128)(2,1)}, bf16[4,256,128]{2,1,0:T(8,128)(2,1)S(1)}, u32[]{:S(2)}, u32[]{:S(2)}) collective-permute-start(bf16[4,256,128]{2,1,0:T(8,128)(2,1)} %bitcast.10), channel_id=1, source_target_pairs={{0,1},{1,2},{2,3},{3,4},{4,5},{5,6},{6,7},{7,8},{8,9},{9,10},{10,1... | collective-permute-start | bytes 786440 | tf_op jit(solution)/shard_map/ppermute | solution.py:250
  8.5 16.6 %collective-permute-start.5 = (bf16[4,256,128]{2,1,0:T(8,128)(2,1)}, bf16[4,256,128]{2,1,0:T(8,128)(2,1)S(1)}, u32[]{:S(2)}, u32[]{:S(2)}) collective-permute-start(bf16[4,256,128]{2,1,0:T(8,128)(2,1)} %bitcast.12), channel_id=1, source_target_pairs={{0,16},{1,17},{2,18},{3,19},{4,20},{5,21},{6,22},{7,23},{8,24},{9,... | collective-permute-start | bytes 786440 | tf_op jit(solution)/shard_map/ppermute | solution.py:249
  13.4 11.4 %collective-permute-start.9 = (bf16[2,128,256]{2,1,0:T(8,128)(2,1)}, bf16[2,128,256]{2,1,0:T(8,128)(2,1)}, u32[]{:S(2)}, u32[]{:S(2)}) collective-permute-start(bf16[2,128,256]{2,1,0:T(8,128)(2,1)} %pad_maximum_fusion), channel_id=1, source_target_pairs={{0,16},{1,17},{2,18},{3,19},{4,20},{5,21},{6,22},{7,23},{8,24},{9,... | collective-permute-start | bytes 393224 | tf_op jit(solution)/shard_map/ppermute | solution.py:249
  13.4 9.6 %collective-permute-start.8 = (bf16[54,128]{1,0:T(8,128)(2,1)S(1)}, bf16[54,128]{1,0:T(8,128)(2,1)S(1)}, u32[]{:S(2)}, u32[]{:S(2)}) collective-permute-start(bf16[54,128]{1,0:T(8,128)(2,1)S(1)} %pad_maximum_fusion.1), channel_id=1, source_target_pairs={{0,16},{1,17},{2,18},{3,19},{4,20},{5,21},{6,22},{7,23},{8,24},{9,... | collective-permute-start | bytes 41480 | tf_op jit(solution)/shard_map/ppermute | solution.py:249
  23.0 23.8 %collective-permute-start = (bf16[4,256,128]{2,1,0:T(8,128)(2,1)}, bf16[4,256,128]{2,1,0:T(8,128)(2,1)S(1)}, u32[]{:S(2)}, u32[]{:S(2)}) collective-permute-start(bf16[4,256,128]{2,1,0:T(8,128)(2,1)} %bitcast.41), channel_id=1, source_target_pairs={{0,16},{1,17},{2,18},{3,19},{4,20},{5,21},{6,22},{7,23},{8,24},{9,... | collective-permute-start | bytes 786440 | tf_op jit(solution)/shard_map/ppermute | solution.py:249
  24.8 11.7 %collective-permute-start.1 = (bf16[4,256,128]{2,1,0:T(8,128)(2,1)}, bf16[4,256,128]{2,1,0:T(8,128)(2,1)}, u32[]{:S(2)}, u32[]{:S(2)}) collective-permute-start(bf16[4,256,128]{2,1,0:T(8,128)(2,1)} %bitcast.6), channel_id=1, source_target_pairs={{0,16},{1,17},{2,18},{3,19},{4,20},{5,21},{6,22},{7,23},{8,24},{9,... | collective-permute-start | bytes 786440 | tf_op jit(solution)/shard_map/ppermute | solution.py:249
  25.1 11.4 %collective-permute-start.7 = (bf16[4,256,128]{2,1,0:T(8,128)(2,1)S(1)}, bf16[4,256,128]{2,1,0:T(8,128)(2,1)}, u32[]{:S(2)}, u32[]{:S(2)}) collective-permute-start(bf16[4,256,128]{2,1,0:T(8,128)(2,1)S(1)} %collective-permute-done.5.rest), channel_id=1, source_target_pairs={{0,1},{1,2},{2,3},{3,4},{4,5},{5,6},{6,7},{7,8},{8,9},{9,10},{10,1... | collective-permute-start | bytes 786440 | tf_op jit(solution)/shard_map/ppermute | solution.py:250
  26.4 31.0 %collective-permute-start.2 = (bf16[4,256,128]{2,1,0:T(8,128)(2,1)}, bf16[4,256,128]{2,1,0:T(8,128)(2,1)S(1)}, u32[]{:S(2)}, u32[]{:S(2)}) collective-permute-start(bf16[4,256,128]{2,1,0:T(8,128)(2,1)} %bitcast.42), channel_id=1, source_target_pairs={{0,1},{1,2},{2,3},{3,4},{4,5},{5,6},{6,7},{7,8},{8,9},{9,10},{10,1... | collective-permute-start | bytes 786440 | tf_op jit(solution)/shard_map/ppermute | solution.py:250
  36.5 20.9 %collective-permute-start.3 = (bf16[4,256,128]{2,1,0:T(8,128)(2,1)}, bf16[4,256,128]{2,1,0:T(8,128)(2,1)S(1)}, u32[]{:S(2)}, u32[]{:S(2)}) collective-permute-start(bf16[4,256,128]{2,1,0:T(8,128)(2,1)} %collective-permute-done.1.rest), channel_id=1, source_target_pairs={{0,1},{1,2},{2,3},{3,4},{4,5},{5,6},{6,7},{7,8},{8,9},{9,10},{10,1... | collective-permute-start | bytes 786440 | tf_op jit(solution)/shard_map/ppermute | solution.py:250
  46.8 6.8 %copy-start.2 = (bf16[16,256,128]{2,1,0:T(8,128)(2,1)}, bf16[16,256,128]{2,1,0:T(8,128)(2,1)S(1)}, u32[]{:S(2)}) copy-start(bf16[16,256,128]{2,1,0:T(8,128)(2,1)S(1)} %get-tuple-element.17.first) | copy-start | bytes 3145732
  47.8 5.7 %copy-start.1 = (bf16[27,256,128]{2,1,0:T(8,128)(2,1)}, bf16[27,256,128]{2,1,0:T(8,128)(2,1)S(1)}, u32[]{:S(2)}) copy-start(bf16[27,256,128]{2,1,0:T(8,128)(2,1)S(1)} %broadcast_in_dim.5.taps) | copy-start | bytes 5308420
  53.7 22.1 %collective-permute-start.16 = (bf16[128,384]{1,0:T(8,128)(2,1)S(1)}, bf16[128,384]{1,0:T(8,128)(2,1)S(1)}, u32[]{:S(2)}, u32[]{:S(2)}) collective-permute-start(bf16[128,384]{1,0:T(8,128)(2,1)S(1)} %fusion.2), channel_id=1, source_target_pairs={{0,16},{1,17},{2,18},{3,19},{4,20},{5,21},{6,22},{7,23},{8,24},{9,... | collective-permute-start | bytes 294920 | tf_op jit(solution)/shard_map/ppermute | solution.py:249
  57.4 13.4 %copy-start = (bf16[27,256,128]{2,1,0:T(8,128)(2,1)S(1)}, bf16[27,256,128]{2,1,0:T(8,128)(2,1)}, u32[]{:S(2)}) copy-start(bf16[27,256,128]{2,1,0:T(8,128)(2,1)} %broadcast_in_dim.4.taps) | copy-start | bytes 5308420
  70.7 5.2 %collective-permute-start.11 = (bf16[128,384]{1,0:T(8,128)(2,1)S(1)}, bf16[128,384]{1,0:T(8,128)(2,1)S(1)}, u32[]{:S(2)}, u32[]{:S(2)}) collective-permute-start(bf16[128,384]{1,0:T(8,128)(2,1)S(1)} %fusion.4), channel_id=1, source_target_pairs={{0,16},{1,17},{2,18},{3,19},{4,20},{5,21},{6,22},{7,23},{8,24},{9,... | collective-permute-start | bytes 294920 | tf_op jit(solution)/shard_map/ppermute | solution.py:249
  73.4 7.6 %collective-permute-start.10 = (bf16[4,256,128]{2,1,0:T(8,128)(2,1)S(1)}, bf16[4,256,128]{2,1,0:T(8,128)(2,1)S(1)}, u32[]{:S(2)}, u32[]{:S(2)}) collective-permute-start(bf16[4,256,128]{2,1,0:T(8,128)(2,1)S(1)} %get-tuple-element.21), channel_id=1, source_target_pairs={{0,16},{1,17},{2,18},{3,19},{4,20},{5,21},{6,22},{7,23},{8,24},{9,... | collective-permute-start | bytes 786440 | tf_op jit(solution)/shard_map/ppermute | solution.py:249
  75.8 1.4 %collective-permute-start.17 = (bf16[128,384]{1,0:T(8,128)(2,1)S(1)}, bf16[128,384]{1,0:T(8,128)(2,1)S(1)}, u32[]{:S(2)}, u32[]{:S(2)}) collective-permute-start(bf16[128,384]{1,0:T(8,128)(2,1)S(1)} %add_convert_fusion.3), channel_id=1, source_target_pairs={{0,1},{1,0},{2,3},{3,2},{4,5},{5,4},{6,7},{7,6},{8,9},{9,8},{10,11... | collective-permute-start | bytes 294920 | tf_op jit(solution)/shard_map/ppermute | solution.py:320
  76.0 1.5 %collective-permute-start.12 = (bf16[128,384]{1,0:T(8,128)(2,1)S(1)}, bf16[128,384]{1,0:T(8,128)(2,1)S(1)}, u32[]{:S(2)}, u32[]{:S(2)}) collective-permute-start(bf16[128,384]{1,0:T(8,128)(2,1)S(1)} %add_convert_fusion.7), channel_id=1, source_target_pairs={{0,1},{1,0},{2,3},{3,2},{4,5},{5,4},{6,7},{7,6},{8,9},{9,8},{10,11... | collective-permute-start | bytes 294920 | tf_op jit(solution)/shard_map/ppermute | solution.py:320
  77.2 5.8 %collective-permute-start.18 = (bf16[128,384]{1,0:T(8,128)(2,1)S(1)}, bf16[128,384]{1,0:T(8,128)(2,1)S(1)}, u32[]{:S(2)}, u32[]{:S(2)}) collective-permute-start(bf16[128,384]{1,0:T(8,128)(2,1)S(1)} %add_convert_fusion.2), channel_id=1, source_target_pairs={{0,2},{1,3},{2,0},{3,1},{4,6},{5,7},{6,4},{7,5},{8,10},{9,11},{10,... | collective-permute-start | bytes 294920 | tf_op jit(solution)/shard_map/ppermute | solution.py:320
  77.5 7.1 %collective-permute-start.13 = (bf16[128,384]{1,0:T(8,128)(2,1)S(1)}, bf16[128,384]{1,0:T(8,128)(2,1)S(1)}, u32[]{:S(2)}, u32[]{:S(2)}) collective-permute-start(bf16[128,384]{1,0:T(8,128)(2,1)S(1)} %add_convert_fusion.6), channel_id=1, source_target_pairs={{0,2},{1,3},{2,0},{3,1},{4,6},{5,7},{6,4},{7,5},{8,10},{9,11},{10,... | collective-permute-start | bytes 294920 | tf_op jit(solution)/shard_map/ppermute | solution.py:320
  83.1 5.4 %collective-permute-start.19 = (bf16[128,384]{1,0:T(8,128)(2,1)S(1)}, bf16[128,384]{1,0:T(8,128)(2,1)S(1)}, u32[]{:S(2)}, u32[]{:S(2)}) collective-permute-start(bf16[128,384]{1,0:T(8,128)(2,1)S(1)} %add_convert_fusion.1), channel_id=1, source_target_pairs={{0,4},{1,5},{2,6},{3,7},{4,0},{5,1},{6,2},{7,3},{8,12},{9,13},{10,... | collective-permute-start | bytes 294920 | tf_op jit(solution)/shard_map/ppermute | solution.py:320
  84.6 6.7 %collective-permute-start.14 = (bf16[128,384]{1,0:T(8,128)(2,1)S(1)}, bf16[128,384]{1,0:T(8,128)(2,1)S(1)}, u32[]{:S(2)}, u32[]{:S(2)}) collective-permute-start(bf16[128,384]{1,0:T(8,128)(2,1)S(1)} %add_convert_fusion.5), channel_id=1, source_target_pairs={{0,4},{1,5},{2,6},{3,7},{4,0},{5,1},{6,2},{7,3},{8,12},{9,13},{10,... | collective-permute-start | bytes 294920 | tf_op jit(solution)/shard_map/ppermute | solution.py:320
  88.5 9.6 %collective-permute-start.20 = (bf16[128,384]{1,0:T(8,128)(2,1)S(1)}, bf16[128,384]{1,0:T(8,128)(2,1)S(1)}, u32[]{:S(2)}, u32[]{:S(2)}) collective-permute-start(bf16[128,384]{1,0:T(8,128)(2,1)S(1)} %add_convert_fusion), channel_id=1, source_target_pairs={{0,8},{1,9},{2,10},{3,11},{4,12},{5,13},{6,14},{7,15},{8,0},{9,1},... | collective-permute-start | bytes 294920 | tf_op jit(solution)/shard_map/ppermute | solution.py:320
  91.3 8.1 %collective-permute-start.15 = (bf16[128,384]{1,0:T(8,128)(2,1)S(1)}, bf16[128,384]{1,0:T(8,128)(2,1)S(1)}, u32[]{:S(2)}, u32[]{:S(2)}) collective-permute-start(bf16[128,384]{1,0:T(8,128)(2,1)S(1)} %add_convert_fusion.4), channel_id=1, source_target_pairs={{0,8},{1,9},{2,10},{3,11},{4,12},{5,13},{6,14},{7,15},{8,0},{9,1},... | collective-permute-start | bytes 294920 | tf_op jit(solution)/shard_map/ppermute | solution.py:320

commit v2 on v0

v2 whole, which is shorter than its diff:
```python
import math

import jax
import jax.numpy as jnp
from jax import lax
from jax.experimental import pallas as pl
from jax.experimental.pallas import tpu as pltpu
from jax.sharding import PartitionSpec as P

AXES = ("own", "space")
BF = jnp.bfloat16
F32 = jnp.float32
TAPS = [
    (9 * (a + 1) + 3 * (b + 1) + (d + 1), a, b, d)
    for a in (-1, 0, 1)
    for b in (-1, 0, 1)
    for d in (-1, 0, 1)
]
LANES = 128
GROUP = 16
MICROSECONDS = {"density": 1, "cotangent": 1, "weights": 1, "stencils": 5, "forward": 5, "second": 4, "backward": 8, "input": 3, "finish": 1}
PLANES = 4
VMEM = pl.BlockSpec(memory_space=pltpu.VMEM)
SMEM = pl.BlockSpec(memory_space=pltpu.SMEM)
HBM = pl.BlockSpec(memory_space=pltpu.HBM)


def tap_index(a, b, d):
    return 9 * (a + 1) + 3 * (b + 1) + (d + 1)


def tree(terms):
    while len(terms) > 1:
        paired = [terms[i] + terms[i + 1] for i in range(0, len(terms) - 1, 2)]
        terms = paired + ([terms[-1]] if len(terms) % 2 else [])
    return terms[0]


def turned(value, shift):
    return pltpu.roll(value, shift % LANES, 1)


def side_by_side(slabs):
    return jnp.concatenate(slabs, axis=1)


def contract(left, right):
    return lax.dot_general(left, right, (((1,), (1,)), ((), ())), preferred_element_type=F32)


def group_rows(group):
    return pl.ds(group * GROUP, GROUP)


def stencil_sums(data, stencil, turn, moved, blocks, emit):
    height = 2 * blocks + 2
    for slab in range(PLANES * height):
        both = jnp.dot(data[slab], turn[...], preferred_element_type=F32).astype(BF)
        moved[0, slab] = both[:, :LANES]
        moved[1, slab] = both[:, LANES:]
    for group in range(data.shape[1] // GROUP):
        rows = group_rows(group)

        def piece(d, x, y):
            return data[x * height + y, rows, :] if d == 1 else moved[d // 2, x * height + y, rows, :]

        columns = [
            jnp.concatenate([piece(d, x, 2 * block + y) for d in range(3) for x in range(PLANES) for y in range(4)], axis=0)
            for block in range(blocks)
        ]
        total = jnp.dot(stencil[group], side_by_side(columns), preferred_element_type=F32)
        for x in range(PLANES):
            for block in range(blocks):
                for y in range(2):
                    start = (x * 2 + y) * GROUP
                    emit(x, 2 * block + y, rows, total[start : start + GROUP, block * LANES : (block + 1) * LANES])


def tap_products(load, gradient, rows, emit):
    turns = {}
    for x in range(PLANES):
        for y in rows:
            value = gradient(x, y)
            wide = value.astype(F32)
            turns[x, y] = {-1: turned(wide, -1).astype(BF), 0: value, 1: turned(wide, 1).astype(BF)}
    for k, a, b, d in TAPS:
        emit(k, tree([load((x + a) % PLANES, y + b) * turns[x, y][d] for x in range(PLANES) for y in rows]))


def tap_sums(load, gradient, rows, products, selector):
    channels = products.shape[0]

    def step(group, carry):
        at = pl.ds(pl.multiple_of(group * GROUP, GROUP), GROUP)

        def keep(k, value):
            products[at, k * LANES : (k + 1) * LANES] = value

        tap_products(lambda x, y: load(x, y, at), lambda x, y: gradient(x, y, at), rows, keep)
        return carry

    lax.fori_loop(0, channels // GROUP, step, 0)
    return jnp.dot(products[...], selector[...], preferred_element_type=F32)


def fetch(source, target, sem):
    copy = pltpu.make_async_copy(source, target, sem)
    copy.start()
    return copy


def rows_of(value, wide, rows):
    for group in range(value.shape[0] // GROUP):
        at = group_rows(group)
        wide[...] = value[at].astype(F32).reshape(GROUP * 8, LANES)
        for row in range(8):
            rows[row, at, :] = wide[pl.ds(row, GROUP, stride=8), :].astype(BF)


def slab_at(index, channels):
    return pl.ds(index * channels, channels)


def density_kernel(
    own_ref, value_far, dw_one_far, dw_two_far, pw_one_far, pw_two_far, rows, strip, rest, rest_more,
    value, dw_one, dw_two, pw_one, pw_two, wide, sems,
):
    own = own_ref[0]
    moves = ((value_far, value), (dw_one_far, dw_one), (dw_two_far, dw_two), (pw_one_far, pw_one), (pw_two_far, pw_two))
    copies = [fetch(source, target, sems.at[index]) for index, (source, target) in enumerate(moves)]
    for copy in copies:
        copy.wait()
    channels = value.shape[0]
    rows_of(value, wide, rows)
    for x in range(2):
        for y in range(2):
            strip[slab_at(x * 2 + y, channels), :] = rows[x * 4 + 2 * own + y]
            piece = rows[x * 4 + 2 - 2 * own + y]
            rest[slab_at(x * 2 + y, channels), :] = piece
            rest_more[slab_at(x * 2 + y, channels), :] = piece
    base = 4 * channels
    strip[base:, :] = jnp.zeros((64, LANES), BF)
    strip[base : base + 27, :] = dw_one[...]
    strip[base + 32 : base + 59, :] = dw_two[...]
    half = channels // 2
    for index, weight in enumerate((pw_one, pw_two)):
        for side in range(2):
            start = base + index * channels + side * half
            rest_more[start : start + half, :] = weight[:, side * LANES : (side + 1) * LANES]


def cotangent_kernel(own_ref, value_far, rows, strip, rest, value, wide, sem):
    own = own_ref[0]
    fetch(value_far, value, sem).wait()
    channels = value.shape[0]
    rows_of(value, wide, rows)
    for x in range(2):
        for y in range(2):
            strip[slab_at(x * 2 + y, channels), :] = rows[x * 4 + 2 * own + y]
            rest[slab_at(x * 2 + y, channels), :] = rows[x * 4 + 2 - 2 * own + y]


def weights_kernel(own_ref, mine, message, weight_one, weight_two, weight_one_t):
    first = own_ref[0] == 0
    channels = weight_one.shape[0]
    half = channels // 2
    base = 4 * channels
    for index, out in enumerate((weight_one, weight_two)):
        start = base + index * channels
        here, other = (
            side_by_side([part[start : start + half, :], part[start + half : start + channels, :]]).astype(F32) for part in (mine, message)
        )
        top, bottom = jnp.where(first, here, other), jnp.where(first, other, here)
        out[:half, :] = top.astype(BF)
        out[half:, :] = bottom.astype(BF)
        if index == 0:
            weight_one_t[:, :half] = top.T.astype(BF)
            weight_one_t[:, half:] = bottom.T.astype(BF)


def stencil_kernel(
    own_ref, mine, message, one_forward, one_back, two_forward, two_back, turn, selector, columns, stencils, sems
):
    first = own_ref[0] == 0
    here, there = (part[part.shape[0] - 64 :, :].astype(F32) for part in (mine, message))
    columns[...] = side_by_side([jnp.where(first, here, there), jnp.where(first, there, here)]).T
    channels = columns.shape[0]
    outs = (one_forward, one_back, two_forward, two_back)
    row = lax.broadcasted_iota(jnp.int32, (GROUP, LANES), 0)
    lane = lax.broadcasted_iota(jnp.int32, (GROUP, LANES), 1)
    diagonal = lane % GROUP == row
    masks = [jnp.logical_and(diagonal, (lane // GROUP) % 4 == j) for j in range(4)]
    low = lane < 4 * GROUP
    zero = jnp.zeros((GROUP, LANES), F32)

    def step(group, carry):
        at = pl.ds(pl.multiple_of(group * GROUP, GROUP), GROUP)
        block = columns[at, :]
        for base, which in ((0, (0, 1)), (32, (2, 3))):
            wide = [jnp.broadcast_to(block[:, base + k : base + k + 1], (GROUP, LANES)) for k in range(27)]
            for index, sign in zip(which, (1, -1)):
                for d in (-1, 0, 1):
                    for y in range(2):
                        strips = {2: zero}
                        for a in (-1, 0, 1):
                            value = zero
                            for b in (-1, 0, 1):
                                value = jnp.where(masks[y + 1 + b], wide[tap_index(sign * a, sign * b, sign * d)], value)
                            strips[a] = value
                        for x in range(PLANES):
                            for half in range(2):
                                left = (2 * half - x + 1) % 4 - 1
                                right = (2 * half + 1 - x + 1) % 4 - 1
                                tile = jnp.where(low, strips[left], strips[right]).astype(BF)
                                start = (d + 1) * 2 * LANES + half * LANES
                                stencils[index, group, (x * 2 + y) * GROUP : (x * 2 + y + 1) * GROUP, start : start + LANES] = tile
        for index, out in enumerate(outs):
            pltpu.make_async_copy(stencils.at[index, group], out.at[group], sems.at[index]).start()
        return carry

    lax.fori_loop(0, channels // GROUP, step, 0)
    source = lax.broadcasted_iota(jnp.int32, (LANES, LANES), 0)
    target = lax.broadcasted_iota(jnp.int32, (LANES, LANES), 1)
    turn[:, :LANES] = (source == (target + LANES - 1) % LANES).astype(F32).astype(BF)
    turn[:, LANES:] = (source == (target + 1) % LANES).astype(F32).astype(BF)
    for k in range(27):
        selector[k * LANES : (k + 1) * LANES, :] = (target == k).astype(F32).astype(BF)
    for index, out in enumerate(outs):
        pltpu.make_async_copy(stencils.at[index], out, sems.at[index]).wait()


def fill_extended(own, ext, local, beside, rest, halo, halo_beside):
    channels = local.shape[1]
    for x in range(2):
        for y in range(4):
            ext[x * 6 + 2 * (1 - own) + y] = local[x * 4 + y]
        for y in range(2):
            at = slab_at(x * 2 + y, channels)
            ext[x * 6 + 4 * own + y] = halo[at, :]
            ext[(x + 2) * 6 + 4 * own + y] = halo_beside[at, :]
            ext[(x + 2) * 6 + 2 + y] = beside[at, :]
            ext[(x + 2) * 6 + 4 * (1 - own) + y] = rest[at, :]


def forward_kernel(
    own_ref, one_source, two_source, local, beside, rest, halo, halo_beside, turn, weight_t, ext, first, act, slope, second,
    one_forward, two_forward, one_sem, two_sem, moved,
):
    channels = local.shape[1]
    one_copy, two_copy = fetch(one_source, one_forward, one_sem), fetch(two_source, two_forward, two_sem)
    fill_extended(own_ref[0], ext, local, beside, rest, halo, halo_beside)
    one_copy.wait()

    def emit(x, y, rows, total):
        first[x * 4 + y, rows, :] = total.astype(BF)

    stencil_sums(ext, one_forward, turn, moved, 2, emit)
    for base in range(0, 16, 4):
        source = side_by_side([first[base + j] for j in range(4)])
        pre = jnp.dot(weight_t[...], source, preferred_element_type=F32)
        sigma = jax.nn.sigmoid(pre)
        value = (pre * sigma).astype(BF)
        factor = (sigma * (1.0 + pre * (1.0 - sigma))).astype(BF)
        for j in range(4):
            act[base + j] = value[:, j * LANES : (j + 1) * LANES]
            slope[base + j] = factor[:, j * LANES : (j + 1) * LANES]

    two_copy.wait()

    def emit_second(x, y, rows, total):
        second[x * 2 + y, rows, :] = total.astype(BF)

    stencil_sums(act, two_forward, turn, moved, 1, emit_second)


def second_kernel(own_ref, act, second, local, beside, weight, selector, grad_pw, grad_dw, cotan, grad_second, products):
    own = own_ref[0]
    channels = act.shape[1]
    for x in range(2):
        for y in range(2):
            cotan[x * 2 + y] = local[x * 4 + 2 * own + y]
            cotan[(x + 2) * 2 + y] = beside[slab_at(x * 2 + y, channels), :]
    for x in range(PLANES):
        source = side_by_side([cotan[x * 2], cotan[x * 2 + 1]])
        value = jnp.dot(weight[...], source, preferred_element_type=F32).astype(BF)
        grad_second[x * 2] = value[:, :LANES]
        grad_second[x * 2 + 1] = value[:, LANES:]
    total = jnp.zeros((channels, channels), F32)
    for x in range(PLANES):
        total += contract(side_by_side([second[2 * x], second[2 * x + 1]]), side_by_side([cotan[2 * x], cotan[2 * x + 1]]))
    grad_pw[...] = total
    grad_dw[...] = tap_sums(
        lambda x, y, rows: act[x * 4 + y, rows, :], lambda x, y, rows: grad_second[x * 2 + y - 1, rows, :], range(1, 3), products, selector
    )


def backward_kernel(
    own_ref, core_ref, two_source, local, beside, rest, halo, halo_beside, slope, first, density, turn, weight_two, weight_one,
    selector, grad_pw_two, grad_dw_two, grad_first, parts, ext, grad_second, grad_pre, products, whole, two_back, two_sem, moved,
):
    core = core_ref[0]
    two_copy = fetch(two_source, two_back, two_sem)
    channels = local.shape[1]
    half = channels // 2
    fill_extended(own_ref[0], ext, local, beside, rest, halo, halo_beside)
    for base in range(0, 24, 4):
        source = side_by_side([ext[base + j] for j in range(4)])
        value = jnp.dot(weight_two[...], source, preferred_element_type=F32).astype(BF)
        for j in range(4):
            grad_second[base + j] = value[:, j * LANES : (j + 1) * LANES]

    two_copy.wait()

    def emit(x, y, rows, total):
        slab = x * 4 + y
        grad_pre[slab, rows, :] = (total * slope[slab, rows, :].astype(F32)).astype(BF)

    stencil_sums(grad_second, two_back, turn, moved, 2, emit)
    for base in range(0, 16, 4):
        source = side_by_side([grad_pre[base + j] for j in range(4)])
        value = jnp.dot(weight_one[...], source, preferred_element_type=F32).astype(BF)
        for j in range(4):
            grad_first[base + j] = value[:, j * LANES : (j + 1) * LANES]
    total = jnp.zeros((channels, channels), F32)
    for x in range(PLANES):
        total += contract(
            side_by_side([first[4 * x + 1], first[4 * x + 2]]), side_by_side([grad_pre[4 * x + 1], grad_pre[4 * x + 2]])
        )
    grad_dw_one = tap_sums(
        lambda x, y, rows: density[x * 6 + y, rows, :], lambda x, y, rows: grad_first[x * 4 + y - 1, rows, :], range(2, 4), products, selector
    )
    dw_one_rows = grad_dw_one.T
    dw_two_rows = grad_dw_two[...].T
    for side in range(2):
        span = slice(side * half, (side + 1) * half)
        whole[side, :half, :] = total[span]
        whole[side, half : 2 * half, :] = grad_pw_two[span, :]
        whole[side, 2 * half :, :half] = dw_one_rows[:32, span]
        whole[side, 2 * half :, half:] = dw_two_rows[:32, span]
    block = parts.shape[2]
    for part in range(2):
        place = part * (1 - core) + (1 - part) * core
        parts[place] = whole[:, part * block : (part + 1) * block, :]


def input_kernel(own_ref, one_source, local, beside, grad_first, turn, mine, other, one_back, one_sem, moved):
    own = own_ref[0]
    fetch(one_source, one_back, one_sem).wait()
    channels = local.shape[1]

    def emit(x, y, rows, total):
        slab = (x % 2) * 2 + y
        if x < 2:
            mine[slab, rows, :] = (local[x * 4 + 2 * own + y, rows, :].astype(F32) + total).astype(BF)
        else:
            at = pl.ds(slab * channels + rows.start, GROUP)
            other[slab, rows, :] = (beside[at, :].astype(F32) + total).astype(BF)

    stencil_sums(grad_first, one_back, turn, moved, 1, emit)


def finish_kernel(scale, core_ref, mine, other, pw_one, pw_two, dw_one, dw_two):
    first = core_ref[0] == 0
    top = jnp.where(first, mine[...], other[...]) * scale
    bottom = jnp.where(first, other[...], mine[...]) * scale
    half = pw_one.shape[0]
    spare = top.shape[0] - half
    pw_one[...] = top[:half]
    pw_two[:spare, :] = top[half:]
    pw_two[spare:, :] = bottom[: half - spare]
    dw_one[...] = bottom[half - spare : half - spare + 27, :half]
    dw_two[...] = bottom[half - spare : half - spare + 27, half:]


def call(kernel, name, outs, scratch, scalars, inputs, limit, far_in=(), far_out=0):
    return pl.pallas_call(
        kernel,
        name=name,
        out_shape=[(pltpu.HBM if i < far_out else jax.ShapeDtypeStruct)(shape, dtype) for i, (shape, dtype) in enumerate(outs)],
        in_specs=[SMEM] * len(scalars) + [HBM] * len(far_in) + [VMEM] * len(inputs),
        out_specs=[HBM] * far_out + [VMEM] * (len(outs) - far_out),
        scratch_shapes=scratch,
        compiler_params=pltpu.CompilerParams(vmem_limit_bytes=limit * 1024 * 1024),
        cost_estimate=pl.CostEstimate(flops=MICROSECONDS[name] * 1_150_000_000, bytes_accessed=1024, transcendentals=0),
    )(*scalars, *[pltpu.with_memory_space_constraint(value, pltpu.HBM) for value in far_in], *inputs)


def shards(density, cotangent, pw_one, pw_two, dw_one, dw_two):
    channels, extent_x, extent_y, extent_z = density.shape
    own_size, space_size = lax.axis_size("own"), lax.axis_size("space")
    own, spot = lax.axis_index("own"), lax.axis_index("space")
    core = spot % 2
    place = lambda o, s: o * space_size + s % space_size
    every = [(o, s) for o in range(own_size) for s in range(space_size)]
    across = [(place(o, s), place(1 - o, s)) for o, s in every]
    onward = [(place(o, s), place(o, s + 1 - 2 * o)) for o, s in every]
    swap = lambda value: lax.ppermute(value, AXES, across)
    pass_on = lambda value: lax.ppermute(value, AXES, onward)
    own_ref = own.astype(jnp.int32).reshape(1)
    core_ref = core.astype(jnp.int32).reshape(1)

    slab = (channels, LANES)

    merged = lambda value: value.reshape(channels, extent_x * extent_y, extent_z)
    wide = pltpu.VMEM((GROUP * 8, LANES), F32)
    whole = pltpu.VMEM((channels, extent_x * extent_y, extent_z), BF)
    density_rows, density_strip, density_rest, density_rest_more = call(
        density_kernel, "density",
        [((8,) + slab, BF), ((4 * channels + 64, LANES), BF), ((4 * channels, LANES), BF), ((6 * channels, LANES), BF)],
        [whole] + [pltpu.VMEM(part.shape, BF) for part in (dw_one, dw_two, pw_one, pw_two)] + [wide, pltpu.SemaphoreType.DMA((5,))],
        (own_ref,), (), 16, far_in=(merged(density), dw_one, dw_two, pw_one, pw_two),
    )
    cot_rows, cot_strip, cot_rest = call(
        cotangent_kernel, "cotangent",
        [((8,) + slab, BF), ((4 * channels, LANES), BF), ((4 * channels, LANES), BF)],
        [whole, wide, pltpu.SemaphoreType.DMA],
        (own_ref,), (), 16, far_in=(merged(cotangent),),
    )
    density_far = swap(density_strip)
    density_beside = swap(density_rest_more)
    density_rest, cot_strip, cot_rest = lax.optimization_barrier((density_rest, cot_strip, cot_rest))
    cot_far = swap(cot_strip)
    density_halo = pass_on(density_rest)
    cot_halo = pass_on(cot_rest)
    density_far, cot_rest = lax.optimization_barrier((density_far, cot_rest))
    density_halo_far = pass_on(density_far)
    cot_beside = swap(cot_rest)
    weight_one, weight_two, weight_one_t = call(
        weights_kernel, "weights", [((channels, channels), BF)] * 3, [],
        (own_ref,), (density_rest_more, density_beside), 16,
    )

    stencil = (channels // GROUP, 8 * GROUP, 48 * GROUP)
    held = pltpu.VMEM(stencil, BF)
    sem = pltpu.SemaphoreType.DMA
    moved = pltpu.VMEM((2, 24) + slab, BF)
    products = pltpu.VMEM((channels, 27 * LANES), BF)
    some = lambda count: pltpu.VMEM((count,) + slab, BF)
    one_forward, one_back, two_forward, two_back, turn, selector = call(
        stencil_kernel, "stencils",
        [(stencil, BF)] * 4 + [((LANES, 2 * LANES), BF), ((27 * LANES, LANES), BF)],
        [pltpu.VMEM((channels, 64), F32), pltpu.VMEM((4,) + stencil, BF), pltpu.SemaphoreType.DMA((4,))],
        (own_ref,), (density_strip, density_far), 32, far_out=4,
    )
    density_ext, first, act, slope, second = call(
        forward_kernel, "forward",
        [((24,) + slab, BF)] + [((16,) + slab, BF)] * 3 + [((8,) + slab, BF)],
        [held, held, sem, sem, moved],
        (own_ref,),
        (density_rows, density_beside, density_far, density_halo, density_halo_far, turn, weight_one_t),
        40, far_in=(one_forward, two_forward),
    )
    cot_far, act = lax.optimization_barrier((cot_far, act))
    cot_halo_far = pass_on(cot_far)
    pw_two_part, dw_two_part = call(
        second_kernel, "second",
        [((channels, channels), F32), ((channels, LANES), F32)],
        [some(8), some(8), products],
        (own_ref,), (act, second, cot_rows, cot_beside, weight_two, selector),
        32,
    )
    block = (channels + 32) // 2
    grad_first, parts = call(
        backward_kernel, "backward",
        [((16,) + slab, BF), ((2, 2, block, channels), F32)],
        [some(24), some(24), some(16), products, pltpu.VMEM((2, 2 * block, channels), F32), held, sem, moved],
        (own_ref, core_ref),
        (cot_rows, cot_beside, cot_far, cot_halo, cot_halo_far, slope, first, density_ext, turn, weight_two, weight_one,
         selector, pw_two_part, dw_two_part),
        40, far_in=(two_back,),
    )
    twin = [(place(o, s), place(o, s ^ 1)) for o, s in every]
    total = parts[0] + lax.ppermute(parts[1], AXES, twin)
    keep = lax.dynamic_index_in_dim(total, own, 0, keepdims=False)
    give = lax.dynamic_index_in_dim(total, 1 - own, 0, keepdims=False)
    mine, other = call(
        input_kernel, "input",
        [((4,) + slab, BF), ((4,) + slab, BF)], [held, sem, moved],
        (own_ref,), (cot_rows, cot_beside, grad_first, turn),
        32, far_in=(one_back,),
    )
    give, other = lax.optimization_barrier((give.astype(BF), other))
    total = keep + swap(give).astype(F32)
    back = swap(other)
    bits = [1 << i for i in range(1, space_size.bit_length() - 1)]
    swapped = list(bits)
    for i in range(0, len(bits) - 1, 2):
        swapped[i], swapped[i + 1] = bits[i + 1], bits[i]
    for even, odd in zip(bits, swapped):
        pairs = [(place(o, s), place(o, s ^ (odd if s % 2 else even))) for o, s in every]
        sent = total.astype(BF)
        total = sent.astype(F32) + lax.ppermute(sent, AXES, pairs).astype(F32)
    back = back.reshape(2, 2, channels, extent_z)
    mine = mine.reshape(2, 2, channels, extent_z)
    rows = jnp.where(own == 0, jnp.concatenate([mine, back], 1), jnp.concatenate([back, mine], 1))
    total, grad_input = lax.optimization_barrier((total, rows.transpose(2, 0, 1, 3)))
    partner = lax.ppermute(total, AXES, twin)
    scale = 1.0 / math.sqrt(float(extent_x * extent_y * extent_z * own_size * space_size))
    half = channels // 2
    grad_pw_one, grad_pw_two, grad_dw_one, grad_dw_two = call(
        lambda *refs: finish_kernel(scale, *refs), "finish",
        [((half, channels), F32)] * 2 + [((27, half), F32)] * 2, [],
        (core_ref,), (total, partner), 8,
    )
    return grad_input, grad_pw_one, grad_pw_two, grad_dw_one, grad_dw_two


def solution(mesh):
    in_specs = (
        P(None, "own", "space", None),
        P(None, "own", "space", None),
        P("own", None),
        P("own", None),
        P(None, "own"),
        P(None, "own"),
    )
    out_specs = (
        P(None, "own", "space", None),
        P("own", None),
        P("own", None),
        P(None, "own"),
        P(None, "own"),
    )
    return jax.shard_map(shards, mesh=mesh, in_specs=in_specs, out_specs=out_specs, check_vma=False)
```

time: 319 us -> 73 us (0.23)
  waiting for transfers between devices: 102 us -> 26.4 us
  blocking collectives: 69.3 us -> 0 us
  other arithmetic: 52 us -> 1.86 us
  Pallas kernels: 0 us -> 30.8 us
  local copies, waits for them, and re-layouts: 31.8 us -> 1.37 us
  matrix products: 17.5 us -> 0 us
  starting transfers between devices: 27.5 us -> 11.5 us
  between operations: 16.4 us -> 0.85 us
    psum x1 -> x0, waiting for transfers between devices: 82.2 us -> none  [shards(): lax.psum((partials[0], partials[1], partials[2], partials[3]), ('own', 's...]
    psum x1 -> x0, blocking collectives: 42.9 us -> none  [shards(): lax.psum((partials[0], partials[1], partials[2], partials[3]), ('own', 's...]
    convert_element_type x10 -> x3, other arithmetic: 36.3 us -> 0.06 us  [shards(): sent = total.astype(BF)]
    pallas_call x0 -> x9, Pallas kernels: none -> 30.8 us  [call(): pl.pallas_call(kernel, name=name, out_shape=[(pltpu.HBM if i < far_out el...]
    all_gather x4 -> x0, blocking collectives: 26.3 us -> none  [the longest x1 12 us: shards(): lax.all_gather(dw_one, 'own', axis=1, tiled=True)]
    dot_general x5 -> x0, matrix products: 17.5 us -> none  [the longest x2 10.3 us: backmap(): jnp.dot(weights, flattened, preferred_element_type=jnp.float32)]
    ppermute x16 -> x15, starting transfers between devices: 27.5 us -> 11.5 us  [the longest x6 10.9 us: shards(): swap = lambda value: lax.ppermute(value, AXES, across)]
    slice x17 -> x0, local copies, waits for them, and re-layouts: 9.01 us -> none  [the longest x9 5.93 us: depthwise(): shifted = jnp.roll(shifted, -direction * d, axis=3).astype(jnp.float32)]
  transfers between devices with their start and end apart: 17 -> 15, of which waited for: 7 -> 10; matrix products, arithmetic and copies ran while one was open for 13% -> 3% of each run, Pallas kernels for 0% -> 28%
where the time goes in v2:
time: 73 us; the launch traced here: 72.8 us
  Pallas kernels  30.8 us (42%)
  waiting for transfers between devices  26.4 us (36%)
  starting transfers between devices  11.5 us (16%)
  other arithmetic  1.86 us (3%)
  local copies, waits for them, and re-layouts  1.37 us (2%)
  between operations  0.85 us (1%)
    pallas_call x9, Pallas kernels, call(): pl.pallas_call(kernel, name=name, out_shape=[(pltpu.HBM if i < far_out el...  30.8 us
    ppermute x6, waiting for transfers between devices, shards(): swap = lambda value: lax.ppermute(value, AXES, across)  11.2 us
    ppermute x6, starting transfers between devices, shards(): swap = lambda value: lax.ppermute(value, AXES, across)  10.9 us
    ppermute x3, waiting for transfers between devices, shards(): total = sent.astype(F32) + lax.ppermute(sent, AXES, pairs).astype(F32)  9.11 us
    ppermute x4, waiting for transfers between devices, shards(): pass_on = lambda value: lax.ppermute(value, AXES, onward)  4.7 us
    transpose x1, other arithmetic, shards(): rows.transpose(2, 0, 1, 3)  1.74 us
  transfers between devices with their start and end apart: 15, of which 10 were waited for; matrix products, arithmetic and copies ran while one was open for 3% of the time, Pallas kernels for 28%

profile of v2, /device:TPU:0, one launch (start us, length us, event | category | flops | bytes accessed | tf_op | source)
XLA Modules:
  0.0 72.8 jit_solution(2111189336761390722)
XLA Ops:
  0.6 1.4 %density.1 = (bf16[8,256,128]{2,1,0:T(8,128)(2,1)S(1)}, bf16[1088,128]{1,0:T(8,128)(2,1)S(1)}, bf16[1024,128]{1,0:T(8,128)(2,1)S(1)}, bf16[1536,128]{1,0:T(8,128)(2,1)S(1)}) custom-call(s32[1]{0:T(128)} %bitcast.own_ref, bf16[256,8,128]{2,1,0:T(8,128)(2,1)} %bitcast.20, bf16[27,128]{1,0:T(8,128)(2,1)} %dw_one_far.1, bf16[27,128]{1,0:T(8,128)(2,1)} %dw_two_far.1, ...), custom_call_target="tpu_custom_call" | custom-call | flops 1150000000 | bytes 1024 | tf_op jit(solution)/shard_map/density/pallas_call | solution.py:376
  2.1 3.0 %collective-permute-start = (bf16[1088,128]{1,0:T(8,128)(2,1)S(1)}, bf16[1088,128]{1,0:T(8,128)(2,1)S(1)}, u32[]{:S(2)}, u32[]{:S(2)}) collective-permute-start(bf16[1088,128]{1,0:T(8,128)(2,1)S(1)} %get-tuple-element.47.mine), channel_id=1, source_target_pairs={{0,16},{1,17},{2,18},{3,19},{4,20},{5,21},{6,22},{7,23},{8,24},{9,... | collective-permute-start | bytes 835592 | tf_op jit(solution)/shard_map/ppermute | solution.py:397
  5.1 0.1 collective-permute-start.3
  5.2 1.3 %cotangent.1 = (bf16[8,256,128]{2,1,0:T(8,128)(2,1)S(1)}, bf16[1024,128]{1,0:T(8,128)(2,1)S(1)}, bf16[1024,128]{1,0:T(8,128)(2,1)S(1)}) custom-call(s32[1]{0:T(128)} %bitcast.own_ref, bf16[256,8,128]{2,1,0:T(8,128)(2,1)} %bitcast.21), custom_call_target="tpu_custom_call" | custom-call | flops 1150000000 | bytes 1024 | tf_op jit(solution)/shard_map/cotangent/pallas_call | solution.py:376
  6.6 0.0 copy-start
  6.6 0.8 %copy-done = bf16[8,256,128]{2,1,0:T(8,128)(2,1)} copy-done((bf16[8,256,128]{2,1,0:T(8,128)(2,1)}, bf16[8,256,128]{2,1,0:T(8,128)(2,1)S(1)}, u32[]{:S(2)}) %copy-start) | copy-done | bytes 524312
  7.4 0.0 collective-permute-start.4
  7.4 5.4 %collective-permute-start.2 = (bf16[1024,128]{1,0:T(8,128)(2,1)S(1)}, bf16[1024,128]{1,0:T(8,128)(2,1)S(1)}, u32[]{:S(2)}, u32[]{:S(2)}) collective-permute-start(bf16[1024,128]{1,0:T(8,128)(2,1)S(1)} %get-tuple-element.56), channel_id=1, source_target_pairs={{0,16},{1,17},{2,18},{3,19},{4,20},{5,21},{6,22},{7,23},{8,24},{9,... | collective-permute-start | bytes 786440 | tf_op jit(solution)/shard_map/ppermute | solution.py:397
  12.7 0.0 collective-permute-start.6
  12.7 0.0 collective-permute-done.message.rest
  12.7 0.0 collective-permute-start.5
  12.7 4.9 %stencils.1 = (bf16[16,128,768]{2,1,0:T(8,128)(2,1)}, bf16[16,128,768]{2,1,0:T(8,128)(2,1)}, bf16[16,128,768]{2,1,0:T(8,128)(2,1)}, bf16[16,128,768]{2,1,0:T(8,1...) custom-call(s32[1]{0:T(128)} %bitcast.own_ref, bf16[1088,128]{1,0:T(8,128)(2,1)S(1)} %get-tuple-element.47.mine, ...), custom_call_target="tpu_custom_call" | custom-call | flops 5750000128 | bytes 1024 | tf_op jit(solution)/shard_map/stencils/pallas_call | solution.py:376
  17.6 3.4 %collective-permute-done.3.message.beside = bf16[1536,128]{1,0:T(8,128)(2,1)S(1)} collective-permute-done((bf16[1536,128]{1,0:T(8,128)(2,1)S(1)}, bf16[1536,128]{1,0:T(8,128)(2,1)S(1)}, u32[]{:S(2)}, u32[]{:S(2)}) %collective-permute-start.3) | collective-permute-done | bytes 393248 | tf_op jit(solution)/shard_map/ppermute | solution.py:397
  21.0 2.1 %collective-permute-start.1 = (bf16[1024,128]{1,0:T(8,128)(2,1)S(1)}, bf16[1024,128]{1,0:T(8,128)(2,1)S(1)}, u32[]{:S(2)}, u32[]{:S(2)}) collective-permute-start(bf16[1024,128]{1,0:T(8,128)(2,1)S(1)} %get-tuple-element.55), channel_id=1, source_target_pairs={{0,16},{1,17},{2,18},{3,19},{4,20},{5,21},{6,22},{7,23},{8,24},{9,... | collective-permute-start | bytes 786440 | tf_op jit(solution)/shard_map/ppermute | solution.py:397
  23.1 0.1 weights.1
  23.2 0.0 collective-permute-done.4.halo
  23.2 1.0 %collective-permute-done.5.halo_beside = bf16[1088,128]{1,0:T(8,128)(2,1)S(1)} collective-permute-done((bf16[1088,128]{1,0:T(8,128)(2,1)S(1)}, bf16[1088,128]{1,0:T(8,128)(2,1)S(1)}, u32[]{:S(2)}, u32[]{:S(2)}) %collective-permute-start.5) | collective-permute-done | bytes 278560 | tf_op jit(solution)/shard_map/ppermute | solution.py:398
  24.2 0.0 copy-start.1
  24.2 6.2 %forward.1 = (bf16[24,256,128]{2,1,0:T(8,128)(2,1)S(1)}, bf16[16,256,128]{2,1,0:T(8,128)(2,1)S(1)}, bf16[16,256,128]{2,1,0:T(8,128)(2,1)S(1)}, bf16[16,256,128]{2,1,0:T(8,128)(2,1)S(1)}, bf16[8,256,128]{2,1,0:T(8,128)(2,1)S(1)}) custom-call(s32[1]{0:T(128)} %bitcast.own_ref, bf16[16,128,768]{2,1,0:T(8,128)(2,1)} %get-tuple-element.57.one_source, ...), custom_call_target="tpu_custom_call" | custom-call | flops 5750000128 | bytes 1024 | tf_op jit(solution)/shard_map/forward/pallas_call | solution.py:376
  30.4 0.0 collective-permute-done.2.rest
  30.5 0.2 collective-permute-start.7
  30.7 0.7 %collective-permute-done.1.beside = bf16[1024,128]{1,0:T(8,128)(2,1)S(1)} collective-permute-done((bf16[1024,128]{1,0:T(8,128)(2,1)S(1)}, bf16[1024,128]{1,0:T(8,128)(2,1)S(1)}, u32[]{:S(2)}, u32[]{:S(2)}) %collective-permute-start.1) | collective-permute-done | bytes 262176 | tf_op jit(solution)/shard_map/ppermute | solution.py:397
  31.4 0.0 copy-done.1
  31.4 4.0 %second.1 = (f32[256,256]{1,0:T(8,128)S(1)}, f32[256,128]{1,0:T(8,128)S(1)}) custom-call(s32[1]{0:T(128)} %bitcast.own_ref, bf16[16,256,128]{2,1,0:T(8,128)(2,1)S(1)} %get-tuple-element.72.act, bf16[8,256,128]{2,1,0:T(8,128)(2,1)S(1)} %get-tuple-element.73.second, bf16[8,256,128]{2,1,0:T(8,128)(2,1)S(1)} %copy-done.1, ...), custom_call_target="tpu_custom_call" | custom-call | flops 4600000000 | bytes 1024 | tf_op jit(solution)/shard_map/second/pallas_call | solution.py:376
  35.4 0.0 collective-permute-done.6.halo
  35.5 3.7 %collective-permute-done.7.halo_beside = bf16[1024,128]{1,0:T(8,128)(2,1)S(1)} collective-permute-done((bf16[1024,128]{1,0:T(8,128)(2,1)S(1)}, bf16[1024,128]{1,0:T(8,128)(2,1)S(1)}, u32[]{:S(2)}, u32[]{:S(2)}) %collective-permute-start.7) | collective-permute-done | bytes 262176 | tf_op jit(solution)/shard_map/ppermute | solution.py:398
  39.2 8.5 %backward.1 = (bf16[16,256,128]{2,1,0:T(8,128)(2,1)S(1)}, f32[2,2,144,256]{3,2,1,0:T(8,128)S(1)}) custom-call(s32[1]{0:T(128)} %bitcast.own_ref, s32[1]{0:T(128)} %bitcast.1.core_ref.refs_0_, bf16[16,128,768]{2,1,0:T(8,128)(2,1)} %get-tuple-element.53.two_source, bf16[8,256,128]{2,1,0:T(8,128)(2,1)S(1)} %copy-done.1, ...), custom_call_target="tpu_custom_call" | custom-call | flops 9200000000 | bytes 1024 | tf_op jit(solution)/shard_map/backward/pallas_call | solution.py:376
  47.7 0.1 collective-permute-start.8
  47.8 3.5 %input.1 = (bf16[4,256,128]{2,1,0:T(8,128)(2,1)S(1)}, bf16[4,256,128]{2,1,0:T(8,128)(2,1)S(1)}) custom-call(s32[1]{0:T(128)} %bitcast.own_ref, bf16[16,128,768]{2,1,0:T(8,128)(2,1)} %get-tuple-element.77.one_source, bf16[8,256,128]{2,1,0:T(8,128)(2,1)S(1)} %copy-done.1, bf16[1024,128]{1,0:T(8,128)(2,1)S(1)} %collective-permute-done.1.beside, ...), custom_call_target="tpu_custom_call" | custom-call | flops 3449999872 | bytes 1024 | tf_op jit(solution)/shard_map/input/pallas_call | solution.py:376
  51.3 0.0 collective-permute-done.8
  51.4 0.1 collective-permute-start.9
  51.5 4.7 %collective-permute-done.9 = bf16[144,256]{1,0:T(8,128)(2,1)S(1)} collective-permute-done((bf16[144,256]{1,0:T(8,128)(2,1)S(1)}, bf16[144,256]{1,0:T(8,128)(2,1)S(1)}, u32[]{:S(2)}, u32[]{:S(2)}) %collective-permute-start.9) | collective-permute-done | bytes 73760 | tf_op jit(solution)/shard_map/ppermute | solution.py:397
  56.2 0.1 collective-permute-start.10
  56.2 4.3 %collective-permute-done.10 = bf16[144,256]{1,0:T(8,128)(2,1)S(1)} collective-permute-done((bf16[144,256]{1,0:T(8,128)(2,1)S(1)}, bf16[144,256]{1,0:T(8,128)(2,1)S(1)}, u32[]{:S(2)}, u32[]{:S(2)}) %collective-permute-start.10) | collective-permute-done | bytes 73760 | tf_op jit(solution)/shard_map/ppermute | solution.py:492
  60.6 0.1 collective-permute-start.11
  60.7 0.4 collective-permute-start.13
  61.0 0.3 copy.11
  61.3 3.7 %collective-permute-done.11 = bf16[144,256]{1,0:T(8,128)(2,1)S(1)} collective-permute-done((bf16[144,256]{1,0:T(8,128)(2,1)S(1)}, bf16[144,256]{1,0:T(8,128)(2,1)S(1)}, u32[]{:S(2)}, u32[]{:S(2)}) %collective-permute-start.11) | collective-permute-done | bytes 73760 | tf_op jit(solution)/shard_map/ppermute | solution.py:492
  65.1 0.1 collective-permute-start.12
  65.1 2.4 %collective-permute-done.13 = bf16[4,256,128]{2,1,0:T(8,128)(2,1)S(1)} collective-permute-done((bf16[4,256,128]{2,1,0:T(8,128)(2,1)S(1)}, bf16[4,256,128]{2,1,0:T(8,128)(2,1)S(1)}, u32[]{:S(2)}, u32[]{:S(2)}) %collective-permute-start.13) | collective-permute-done | bytes 262176 | tf_op jit(solution)/shard_map/ppermute | solution.py:397
  67.5 0.3 copy.12
  67.8 1.7 %fusion = bf16[256,2,4,128]{3,2,1,0:T(4,128)(2,1)} fusion(bf16[2,2,256,128]{3,1,0,2:T(2,128)(2,1)S(1)} %copy.12, bf16[2,2,256,128]{3,1,0,2:T(2,128)(2,1)S(1)} %copy.11, pred[]{:T(512)S(6)} %eq.5), kind=kLoop, calls=%fused_computation.1 | loop fusion | flops 2359296 | bytes 1048577 | tf_op jit(solution)/shard_map/transpose | solution.py:496
  69.5 1.1 %collective-permute-done.12 = bf16[144,256]{1,0:T(8,128)(2,1)S(1)} collective-permute-done((bf16[144,256]{1,0:T(8,128)(2,1)S(1)}, bf16[144,256]{1,0:T(8,128)(2,1)S(1)}, u32[]{:S(2)}, u32[]{:S(2)}) %collective-permute-start.12) | collective-permute-done | bytes 73760 | tf_op jit(solution)/shard_map/ppermute | solution.py:492
  70.6 0.1 collective-permute-start.14
  70.7 1.4 %collective-permute-done.14.refs_2_ = f32[144,256]{1,0:T(8,128)S(1)} collective-permute-done((f32[144,256]{1,0:T(8,128)S(1)}, f32[144,256]{1,0:T(8,128)S(1)}, u32[]{:S(2)}, u32[]{:S(2)}) %collective-permute-start.14) | collective-permute-done | bytes 147488 | tf_op jit(solution)/shard_map/ppermute | solution.py:497
  72.1 0.7 finish.1
  (7 shorter events, 0.2 us)
Async XLA Ops:
  2.1 10.6 %collective-permute-start = (bf16[1088,128]{1,0:T(8,128)(2,1)S(1)}, bf16[1088,128]{1,0:T(8,128)(2,1)S(1)}, u32[]{:S(2)}, u32[]{:S(2)}) collective-permute-start(bf16[1088,128]{1,0:T(8,128)(2,1)S(1)} %get-tuple-element.47.mine), channel_id=1, source_target_pairs={{0,16},{1,17},{2,18},{3,19},{4,20},{5,21},{6,22},{7,23},{8,24},{9,... | collective-permute-start | bytes 835592 | tf_op jit(solution)/shard_map/ppermute | solution.py:397
  5.1 15.9 %collective-permute-start.3 = (bf16[1536,128]{1,0:T(8,128)(2,1)S(1)}, bf16[1536,128]{1,0:T(8,128)(2,1)S(1)}, u32[]{:S(2)}, u32[]{:S(2)}) collective-permute-start(bf16[1536,128]{1,0:T(8,128)(2,1)S(1)} %get-tuple-element.60.mine), channel_id=1, source_target_pairs={{0,16},{1,17},{2,18},{3,19},{4,20},{5,21},{6,22},{7,23},{8,24},{9,... | collective-permute-start | bytes 1179656 | tf_op jit(solution)/shard_map/ppermute | solution.py:397
  6.6 0.8 %copy-start = (bf16[8,256,128]{2,1,0:T(8,128)(2,1)}, bf16[8,256,128]{2,1,0:T(8,128)(2,1)S(1)}, u32[]{:S(2)}) copy-start(bf16[8,256,128]{2,1,0:T(8,128)(2,1)S(1)} %get-tuple-element.54.local) | copy-start | bytes 1572868
  7.4 15.9 %collective-permute-start.4 = (bf16[1024,128]{1,0:T(8,128)(2,1)S(1)}, bf16[1024,128]{1,0:T(8,128)(2,1)S(1)}, u32[]{:S(2)}, u32[]{:S(2)}) collective-permute-start(bf16[1024,128]{1,0:T(8,128)(2,1)S(1)} %get-tuple-element.61), channel_id=1, source_target_pairs={{0,1},{1,2},{2,3},{3,4},{4,5},{5,6},{6,7},{7,8},{8,9},{9,10},{10,1... | collective-permute-start | bytes 786440 | tf_op jit(solution)/shard_map/ppermute | solution.py:398
  7.4 23.1 %collective-permute-start.2 = (bf16[1024,128]{1,0:T(8,128)(2,1)S(1)}, bf16[1024,128]{1,0:T(8,128)(2,1)S(1)}, u32[]{:S(2)}, u32[]{:S(2)}) collective-permute-start(bf16[1024,128]{1,0:T(8,128)(2,1)S(1)} %get-tuple-element.56), channel_id=1, source_target_pairs={{0,16},{1,17},{2,18},{3,19},{4,20},{5,21},{6,22},{7,23},{8,24},{9,... | collective-permute-start | bytes 786440 | tf_op jit(solution)/shard_map/ppermute | solution.py:397
  12.7 22.7 %collective-permute-start.6 = (bf16[1024,128]{1,0:T(8,128)(2,1)S(1)}, bf16[1024,128]{1,0:T(8,128)(2,1)S(1)}, u32[]{:S(2)}, u32[]{:S(2)}) collective-permute-start(bf16[1024,128]{1,0:T(8,128)(2,1)S(1)} %get-tuple-element.55), channel_id=1, source_target_pairs={{0,1},{1,2},{2,3},{3,4},{4,5},{5,6},{6,7},{7,8},{8,9},{9,10},{10,1... | collective-permute-start | bytes 786440 | tf_op jit(solution)/shard_map/ppermute | solution.py:398
  12.7 11.5 %collective-permute-start.5 = (bf16[1088,128]{1,0:T(8,128)(2,1)S(1)}, bf16[1088,128]{1,0:T(8,128)(2,1)S(1)}, u32[]{:S(2)}, u32[]{:S(2)}) collective-permute-start(bf16[1088,128]{1,0:T(8,128)(2,1)S(1)} %collective-permute-done.message.rest), channel_id=1, source_target_pairs={{0,1},{1,2},{2,3},{3,4},{4,5},{5,6},{6,7},{7,8},{8,9},{9,10},{10,1... | collective-permute-start | bytes 835592 | tf_op jit(solution)/shard_map/ppermute | solution.py:398
  21.0 10.4 %collective-permute-start.1 = (bf16[1024,128]{1,0:T(8,128)(2,1)S(1)}, bf16[1024,128]{1,0:T(8,128)(2,1)S(1)}, u32[]{:S(2)}, u32[]{:S(2)}) collective-permute-start(bf16[1024,128]{1,0:T(8,128)(2,1)S(1)} %get-tuple-element.55), channel_id=1, source_target_pairs={{0,16},{1,17},{2,18},{3,19},{4,20},{5,21},{6,22},{7,23},{8,24},{9,... | collective-permute-start | bytes 786440 | tf_op jit(solution)/shard_map/ppermute | solution.py:397
  24.2 7.3 %copy-start.1 = (bf16[8,256,128]{2,1,0:T(8,128)(2,1)S(1)}, bf16[8,256,128]{2,1,0:T(8,128)(2,1)}, u32[]{:S(2)}) copy-start(bf16[8,256,128]{2,1,0:T(8,128)(2,1)} %copy-done) | copy-start | bytes 1572868
  30.5 8.7 %collective-permute-start.7 = (bf16[1024,128]{1,0:T(8,128)(2,1)S(1)}, bf16[1024,128]{1,0:T(8,128)(2,1)S(1)}, u32[]{:S(2)}, u32[]{:S(2)}) collective-permute-start(bf16[1024,128]{1,0:T(8,128)(2,1)S(1)} %collective-permute-done.2.rest), channel_id=1, source_target_pairs={{0,1},{1,2},{2,3},{3,4},{4,5},{5,6},{6,7},{7,8},{8,9},{9,10},{10,1... | collective-permute-start | bytes 786440 | tf_op jit(solution)/shard_map/ppermute | solution.py:398
  47.7 3.6 %collective-permute-start.8 = (f32[2,144,256]{2,1,0:T(8,128)S(1)}, f32[2,144,256]{2,1,0:T(8,128)S(1)}, u32[]{:S(2)}, u32[]{:S(2)}) collective-permute-start(f32[2,144,256]{2,1,0:T(8,128)S(1)} %slice_bitcast_fusion), channel_id=1, source_target_pairs={{0,1},{1,0},{2,3},{3,2},{4,5},{5,4},{6,7},{7,6},{8,9},{9,8},{10,11... | collective-permute-start | bytes 884744 | tf_op jit(solution)/shard_map/ppermute | solution.py:473
  51.4 4.7 %collective-permute-start.9 = (bf16[144,256]{1,0:T(8,128)(2,1)S(1)}, bf16[144,256]{1,0:T(8,128)(2,1)S(1)}, u32[]{:S(2)}, u32[]{:S(2)}) collective-permute-start(bf16[144,256]{1,0:T(8,128)(2,1)S(1)} %fusion.2), channel_id=1, source_target_pairs={{0,16},{1,17},{2,18},{3,19},{4,20},{5,21},{6,22},{7,23},{8,24},{9,... | collective-permute-start | bytes 221192 | tf_op jit(solution)/shard_map/ppermute | solution.py:397
  56.2 4.4 %collective-permute-start.10 = (bf16[144,256]{1,0:T(8,128)(2,1)S(1)}, bf16[144,256]{1,0:T(8,128)(2,1)S(1)}, u32[]{:S(2)}, u32[]{:S(2)}) collective-permute-start(bf16[144,256]{1,0:T(8,128)(2,1)S(1)} %fusion.1), channel_id=1, source_target_pairs={{0,2},{1,5},{2,0},{3,7},{4,6},{5,1},{6,4},{7,3},{8,10},{9,13},{10,... | collective-permute-start | bytes 221192 | tf_op jit(solution)/shard_map/ppermute | solution.py:492
  60.6 4.4 %collective-permute-start.11 = (bf16[144,256]{1,0:T(8,128)(2,1)S(1)}, bf16[144,256]{1,0:T(8,128)(2,1)S(1)}, u32[]{:S(2)}, u32[]{:S(2)}) collective-permute-start(bf16[144,256]{1,0:T(8,128)(2,1)S(1)} %add_convert_fusion.1), channel_id=1, source_target_pairs={{0,4},{1,3},{2,6},{3,1},{4,0},{5,7},{6,2},{7,5},{8,12},{9,11},{10,... | collective-permute-start | bytes 221192 | tf_op jit(solution)/shard_map/ppermute | solution.py:492
  60.7 6.8 %collective-permute-start.13 = (bf16[4,256,128]{2,1,0:T(8,128)(2,1)S(1)}, bf16[4,256,128]{2,1,0:T(8,128)(2,1)S(1)}, u32[]{:S(2)}, u32[]{:S(2)}) collective-permute-start(bf16[4,256,128]{2,1,0:T(8,128)(2,1)S(1)} %get-tuple-element.82), channel_id=1, source_target_pairs={{0,16},{1,17},{2,18},{3,19},{4,20},{5,21},{6,22},{7,23},{8,24},{9,... | collective-permute-start | bytes 786440 | tf_op jit(solution)/shard_map/ppermute | solution.py:397
  65.1 5.5 %collective-permute-start.12 = (bf16[144,256]{1,0:T(8,128)(2,1)S(1)}, bf16[144,256]{1,0:T(8,128)(2,1)S(1)}, u32[]{:S(2)}, u32[]{:S(2)}) collective-permute-start(bf16[144,256]{1,0:T(8,128)(2,1)S(1)} %add_convert_fusion), channel_id=1, source_target_pairs={{0,8},{1,9},{2,10},{3,11},{4,12},{5,13},{6,14},{7,15},{8,0},{9,1},... | collective-permute-start | bytes 221192 | tf_op jit(solution)/shard_map/ppermute | solution.py:492
  70.6 1.4 %collective-permute-start.14 = (f32[144,256]{1,0:T(8,128)S(1)}, f32[144,256]{1,0:T(8,128)S(1)}, u32[]{:S(2)}, u32[]{:S(2)}) collective-permute-start(f32[144,256]{1,0:T(8,128)S(1)} %convert_add_fusion.refs_1_), channel_id=1, source_target_pairs={{0,1},{1,0},{2,3},{3,2},{4,5},{5,4},{6,7},{7,6},{8,9},{9,8},{10,11... | collective-permute-start | bytes 442376 | tf_op jit(solution)/shard_map/ppermute | solution.py:497

commit v3 on v2

--- a/solution.py
+++ b/solution.py
@@ -18,7 +18,7 @@
 ]
 LANES = 128
 GROUP = 16
-MICROSECONDS = {"density": 1, "cotangent": 1, "weights": 1, "stencils": 5, "forward": 5, "second": 4, "backward": 8, "input": 3, "finish": 1}
+MICROSECONDS = {"density": 1, "cotangent": 1, "weights": 1, "stencils": 5, "forward": 0, "later": 0, "second": 4, "backward": 8, "input": 3, "finish": 1, "assemble": 0}
 PLANES = 4
 VMEM = pl.BlockSpec(memory_space=pltpu.VMEM)
 SMEM = pl.BlockSpec(memory_space=pltpu.SMEM)
@@ -80,11 +80,10 @@
     turns = {}
     for x in range(PLANES):
         for y in rows:
-            value = gradient(x, y)
-            wide = value.astype(F32)
-            turns[x, y] = {-1: turned(wide, -1).astype(BF), 0: value, 1: turned(wide, 1).astype(BF)}
+            wide = gradient(x, y).astype(F32)
+            turns[x, y] = {-1: turned(wide, -1), 0: wide, 1: turned(wide, 1)}
     for k, a, b, d in TAPS:
-        emit(k, tree([load((x + a) % PLANES, y + b) * turns[x, y][d] for x in range(PLANES) for y in rows]))
+        emit(k, tree([load((x + a) % PLANES, y + b).astype(F32) * turns[x, y][d] for x in range(PLANES) for y in rows]))
 
 
 def tap_sums(load, gradient, rows, products, selector):
@@ -94,7 +93,7 @@
         at = pl.ds(pl.multiple_of(group * GROUP, GROUP), GROUP)
 
         def keep(k, value):
-            products[at, k * LANES : (k + 1) * LANES] = value
+            products[at, k * LANES : (k + 1) * LANES] = value.astype(BF)
 
         tap_products(lambda x, y: load(x, y, at), lambda x, y: gradient(x, y, at), rows, keep)
         return carry
@@ -122,7 +121,7 @@
 
 
 def density_kernel(
-    own_ref, value_far, dw_one_far, dw_two_far, pw_one_far, pw_two_far, rows, strip, rest, rest_more,
+    own_ref, core_ref, value_far, dw_one_far, dw_two_far, pw_one_far, pw_two_far, rows, strip, rest, rest_more, weights,
     value, dw_one, dw_two, pw_one, pw_two, wide, sems,
 ):
     own = own_ref[0]
@@ -145,30 +144,34 @@
     half = channels // 2
     for index, weight in enumerate((pw_one, pw_two)):
         for side in range(2):
-            start = base + index * channels + side * half
-            rest_more[start : start + half, :] = weight[:, side * LANES : (side + 1) * LANES]
-
-
-def cotangent_kernel(own_ref, value_far, rows, strip, rest, value, wide, sem):
+            start = index * channels + side * half
+            weights[start : start + half, :] = weight[:, side * LANES : (side + 1) * LANES]
+    rest_more[base:, :] = weights[pl.ds(core_ref[0] * channels, channels), :]
+
+
+def cotangent_kernel(own_ref, value_far, more, rows, message, rest, value, wide, sem):
     own = own_ref[0]
-    fetch(value_far, value, sem).wait()
+    copy = fetch(value_far, value, sem)
     channels = value.shape[0]
+    message[4 * channels :, :] = more[...]
+    copy.wait()
     rows_of(value, wide, rows)
     for x in range(2):
         for y in range(2):
-            strip[slab_at(x * 2 + y, channels), :] = rows[x * 4 + 2 * own + y]
+            message[slab_at(x * 2 + y, channels), :] = rows[x * 4 + 2 * own + y]
             rest[slab_at(x * 2 + y, channels), :] = rows[x * 4 + 2 - 2 * own + y]
 
 
-def weights_kernel(own_ref, mine, message, weight_one, weight_two, weight_one_t):
+def weights_kernel(own_ref, core_ref, mine, beside, twin, weight_one, weight_two, weight_one_t):
     first = own_ref[0] == 0
+    straight = core_ref[0] == 0
     channels = weight_one.shape[0]
     half = channels // 2
-    base = 4 * channels
     for index, out in enumerate((weight_one, weight_two)):
-        start = base + index * channels
+        a, b = (part[...].astype(F32) for part in ((beside, twin) if index == 0 else (twin, beside)))
         here, other = (
-            side_by_side([part[start : start + half, :], part[start + half : start + channels, :]]).astype(F32) for part in (mine, message)
+            side_by_side([part[:half], part[half:]])
+            for part in (mine[index * channels : (index + 1) * channels, :].astype(F32), jnp.where(straight, a, b))
         )
         top, bottom = jnp.where(first, here, other), jnp.where(first, other, here)
         out[:half, :] = top.astype(BF)
@@ -179,13 +182,14 @@
 
 
 def stencil_kernel(
-    own_ref, mine, message, one_forward, one_back, two_forward, two_back, turn, selector, columns, stencils, sems
+    own_ref, mine, message, one_back, two_back, one_forward, two_forward, turn, selector, columns, stencils, sems
 ):
     first = own_ref[0] == 0
     here, there = (part[part.shape[0] - 64 :, :].astype(F32) for part in (mine, message))
     columns[...] = side_by_side([jnp.where(first, here, there), jnp.where(first, there, here)]).T
     channels = columns.shape[0]
-    outs = (one_forward, one_back, two_forward, two_back)
+    outs = (one_back, two_back)
+    targets = [one_forward, two_forward] + [stencils.at[index] for index in range(2)]
     row = lax.broadcasted_iota(jnp.int32, (GROUP, LANES), 0)
     lane = lax.broadcasted_iota(jnp.int32, (GROUP, LANES), 1)
     diagonal = lane % GROUP == row
@@ -196,7 +200,7 @@
     def step(group, carry):
         at = pl.ds(pl.multiple_of(group * GROUP, GROUP), GROUP)
         block = columns[at, :]
-        for base, which in ((0, (0, 1)), (32, (2, 3))):
+        for base, which in ((0, (0, 2)), (32, (1, 3))):
             wide = [jnp.broadcast_to(block[:, base + k : base + k + 1], (GROUP, LANES)) for k in range(27)]
             for index, sign in zip(which, (1, -1)):
                 for d in (-1, 0, 1):
@@ -213,7 +217,7 @@
                                 right = (2 * half + 1 - x + 1) % 4 - 1
                                 tile = jnp.where(low, strips[left], strips[right]).astype(BF)
                                 start = (d + 1) * 2 * LANES + half * LANES
-                                stencils[index, group, (x * 2 + y) * GROUP : (x * 2 + y + 1) * GROUP, start : start + LANES] = tile
+                                targets[index][group, (x * 2 + y) * GROUP : (x * 2 + y + 1) * GROUP, start : start + LANES] = tile
         for index, out in enumerate(outs):
             pltpu.make_async_copy(stencils.at[index, group], out.at[group], sems.at[index]).start()
         return carry
@@ -229,7 +233,7 @@
         pltpu.make_async_copy(stencils.at[index], out, sems.at[index]).wait()
 
 
-def fill_extended(own, ext, local, beside, rest, halo, halo_beside):
+def fill_extended(own, ext, local, beside, rest, halo, halo_beside, beside_base=0):
     channels = local.shape[1]
     for x in range(2):
         for y in range(4):
@@ -238,18 +242,14 @@
             at = slab_at(x * 2 + y, channels)
             ext[x * 6 + 4 * own + y] = halo[at, :]
             ext[(x + 2) * 6 + 4 * own + y] = halo_beside[at, :]
-            ext[(x + 2) * 6 + 2 + y] = beside[at, :]
+            ext[(x + 2) * 6 + 2 + y] = beside[pl.ds(beside_base + (x * 2 + y) * channels, channels), :]
             ext[(x + 2) * 6 + 4 * (1 - own) + y] = rest[at, :]
 
 
 def forward_kernel(
-    own_ref, one_source, two_source, local, beside, rest, halo, halo_beside, turn, weight_t, ext, first, act, slope, second,
-    one_forward, two_forward, one_sem, two_sem, moved,
+    own_ref, local, beside, rest, halo, halo_beside, one_forward, turn, weight_t, ext, first, act, slope, moved
 ):
-    channels = local.shape[1]
-    one_copy, two_copy = fetch(one_source, one_forward, one_sem), fetch(two_source, two_forward, two_sem)
-    fill_extended(own_ref[0], ext, local, beside, rest, halo, halo_beside)
-    one_copy.wait()
+    fill_extended(own_ref[0], ext, local, beside, rest, halo, halo_beside, beside_base=4 * local.shape[1])
 
     def emit(x, y, rows, total):
         first[x * 4 + y, rows, :] = total.astype(BF)
@@ -258,19 +258,20 @@
     for base in range(0, 16, 4):
         source = side_by_side([first[base + j] for j in range(4)])
         pre = jnp.dot(weight_t[...], source, preferred_element_type=F32)
-        sigma = jax.nn.sigmoid(pre)
+        sigma = 0.5 * jnp.tanh(0.5 * pre) + 0.5
         value = (pre * sigma).astype(BF)
         factor = (sigma * (1.0 + pre * (1.0 - sigma))).astype(BF)
         for j in range(4):
             act[base + j] = value[:, j * LANES : (j + 1) * LANES]
             slope[base + j] = factor[:, j * LANES : (j + 1) * LANES]
 
-    two_copy.wait()
-
-    def emit_second(x, y, rows, total):
+
+def later_kernel(act, two_forward, turn, second, moved):
+
+    def emit(x, y, rows, total):
         second[x * 2 + y, rows, :] = total.astype(BF)
 
-    stencil_sums(act, two_forward, turn, moved, 1, emit_second)
+    stencil_sums(act, two_forward, turn, moved, 1, emit)
 
 
 def second_kernel(own_ref, act, second, local, beside, weight, selector, grad_pw, grad_dw, cotan, grad_second, products):
@@ -359,6 +360,18 @@
     stencil_sums(grad_first, one_back, turn, moved, 1, emit)
 
 
+def assemble_kernel(own_ref, mine, back, out, wide):
+    own = own_ref[0]
+    channels = out.shape[0]
+    for group in range(channels // GROUP):
+        at = group_rows(group)
+        for x in range(2):
+            for y in range(2):
+                wide[pl.ds(x * 4 + 2 * own + y, GROUP, stride=8), :] = mine[x * 2 + y, at, :].astype(F32)
+                wide[pl.ds(x * 4 + 2 - 2 * own + y, GROUP, stride=8), :] = back[x * 2 + y, at, :].astype(F32)
+        out[at] = wide[...].reshape(GROUP, 8, LANES).astype(BF)
+
+
 def finish_kernel(scale, core_ref, mine, other, pw_one, pw_two, dw_one, dw_two):
     first = core_ref[0] == 0
     top = jnp.where(first, mine[...], other[...]) * scale
@@ -404,54 +417,58 @@
     merged = lambda value: value.reshape(channels, extent_x * extent_y, extent_z)
     wide = pltpu.VMEM((GROUP * 8, LANES), F32)
     whole = pltpu.VMEM((channels, extent_x * extent_y, extent_z), BF)
-    density_rows, density_strip, density_rest, density_rest_more = call(
+    density_rows, density_strip, density_rest, density_rest_more, pw_mine = call(
         density_kernel, "density",
-        [((8,) + slab, BF), ((4 * channels + 64, LANES), BF), ((4 * channels, LANES), BF), ((6 * channels, LANES), BF)],
+        [((8,) + slab, BF), ((4 * channels + 64, LANES), BF), ((4 * channels, LANES), BF), ((5 * channels, LANES), BF), ((2 * channels, LANES), BF)],
         [whole] + [pltpu.VMEM(part.shape, BF) for part in (dw_one, dw_two, pw_one, pw_two)] + [wide, pltpu.SemaphoreType.DMA((5,))],
-        (own_ref,), (), 16, far_in=(merged(density), dw_one, dw_two, pw_one, pw_two),
-    )
-    cot_rows, cot_strip, cot_rest = call(
+        (own_ref, core_ref), (), 16, far_in=(merged(density), dw_one, dw_two, pw_one, pw_two),
+    )
+    cot_rows, message, cot_rest = call(
         cotangent_kernel, "cotangent",
-        [((8,) + slab, BF), ((4 * channels, LANES), BF), ((4 * channels, LANES), BF)],
+        [((8,) + slab, BF), ((9 * channels, LANES), BF), ((4 * channels, LANES), BF)],
         [whole, wide, pltpu.SemaphoreType.DMA],
-        (own_ref,), (), 16, far_in=(merged(cotangent),),
+        (own_ref,), (density_rest_more,), 16, far_in=(merged(cotangent),),
     )
     density_far = swap(density_strip)
-    density_beside = swap(density_rest_more)
-    density_rest, cot_strip, cot_rest = lax.optimization_barrier((density_rest, cot_strip, cot_rest))
-    cot_far = swap(cot_strip)
+    density_rest, message = lax.optimization_barrier((density_rest, message))
+    message = swap(message)
     density_halo = pass_on(density_rest)
-    cot_halo = pass_on(cot_rest)
     density_far, cot_rest = lax.optimization_barrier((density_far, cot_rest))
     density_halo_far = pass_on(density_far)
     cot_beside = swap(cot_rest)
-    weight_one, weight_two, weight_one_t = call(
-        weights_kernel, "weights", [((channels, channels), BF)] * 3, [],
-        (own_ref,), (density_rest_more, density_beside), 16,
-    )
-
     stencil = (channels // GROUP, 8 * GROUP, 48 * GROUP)
     held = pltpu.VMEM(stencil, BF)
     sem = pltpu.SemaphoreType.DMA
     moved = pltpu.VMEM((2, 24) + slab, BF)
     products = pltpu.VMEM((channels, 27 * LANES), BF)
     some = lambda count: pltpu.VMEM((count,) + slab, BF)
-    one_forward, one_back, two_forward, two_back, turn, selector = call(
+    one_back, two_back, one_forward, two_forward, turn, selector = call(
         stencil_kernel, "stencils",
         [(stencil, BF)] * 4 + [((LANES, 2 * LANES), BF), ((27 * LANES, LANES), BF)],
-        [pltpu.VMEM((channels, 64), F32), pltpu.VMEM((4,) + stencil, BF), pltpu.SemaphoreType.DMA((4,))],
-        (own_ref,), (density_strip, density_far), 32, far_out=4,
-    )
-    density_ext, first, act, slope, second = call(
+        [pltpu.VMEM((channels, 64), F32), pltpu.VMEM((2,) + stencil, BF), pltpu.SemaphoreType.DMA((2,))],
+        (own_ref,), (density_strip, density_far), 32, far_out=2,
+    )
+    cot_rest, turn = lax.optimization_barrier((cot_rest, turn))
+    message, turn = lax.optimization_barrier((message, turn))
+    cot_far = message[: 4 * channels]
+    cot_halo_far = pass_on(cot_far)
+    cot_halo = pass_on(cot_rest)
+    twin = [(place(o, s), place(o, s ^ 1)) for o, s in every]
+    pw_beside = message[8 * channels :]
+    pw_twin = lax.ppermute(pw_beside, AXES, twin)
+    weight_one, weight_two, weight_one_t = call(
+        weights_kernel, "weights", [((channels, channels), BF)] * 3, [],
+        (own_ref, core_ref), (pw_mine, pw_beside, pw_twin), 16,
+    )
+
+    density_ext, first, act, slope = call(
         forward_kernel, "forward",
-        [((24,) + slab, BF)] + [((16,) + slab, BF)] * 3 + [((8,) + slab, BF)],
-        [held, held, sem, sem, moved],
+        [((24,) + slab, BF)] + [((16,) + slab, BF)] * 3, [moved],
         (own_ref,),
-        (density_rows, density_beside, density_far, density_halo, density_halo_far, turn, weight_one_t),
-        40, far_in=(one_forward, two_forward),
-    )
-    cot_far, act = lax.optimization_barrier((cot_far, act))
-    cot_halo_far = pass_on(cot_far)
+        (density_rows, message, density_far, density_halo, density_halo_far, one_forward, turn, weight_one_t),
+        40,
+    )
+    (second,) = call(later_kernel, "later", [((8,) + slab, BF)], [moved], (), (act, two_forward, turn), 32)
     pw_two_part, dw_two_part = call(
         second_kernel, "second",
         [((channels, channels), F32), ((channels, LANES), F32)],
@@ -469,19 +486,17 @@
          selector, pw_two_part, dw_two_part),
         40, far_in=(two_back,),
     )
-    twin = [(place(o, s), place(o, s ^ 1)) for o, s in every]
     total = parts[0] + lax.ppermute(parts[1], AXES, twin)
     keep = lax.dynamic_index_in_dim(total, own, 0, keepdims=False)
     give = lax.dynamic_index_in_dim(total, 1 - own, 0, keepdims=False)
+    total = keep + swap(give.astype(BF)).astype(F32)
+    total, grad_first = lax.optimization_barrier((total, grad_first))
     mine, other = call(
         input_kernel, "input",
         [((4,) + slab, BF), ((4,) + slab, BF)], [held, sem, moved],
         (own_ref,), (cot_rows, cot_beside, grad_first, turn),
         32, far_in=(one_back,),
     )
-    give, other = lax.optimization_barrier((give.astype(BF), other))
-    total = keep + swap(give).astype(F32)
-    back = swap(other)
     bits = [1 << i for i in range(1, space_size.bit_length() - 1)]
     swapped = list(bits)
     for i in range(0, len(bits) - 1, 2):
@@ -489,11 +504,14 @@
     for even, odd in zip(bits, swapped):
         pairs = [(place(o, s), place(o, s ^ (odd if s % 2 else even))) for o, s in every]
         sent = total.astype(BF)
+        if even == bits[1]:
+            sent, other = lax.optimization_barrier((sent, other))
+            back = swap(other)
         total = sent.astype(F32) + lax.ppermute(sent, AXES, pairs).astype(F32)
-    back = back.reshape(2, 2, channels, extent_z)
-    mine = mine.reshape(2, 2, channels, extent_z)
-    rows = jnp.where(own == 0, jnp.concatenate([mine, back], 1), jnp.concatenate([back, mine], 1))
-    total, grad_input = lax.optimization_barrier((total, rows.transpose(2, 0, 1, 3)))
+    (grad_input,) = call(
+        assemble_kernel, "assemble", [((channels, extent_x * extent_y, extent_z), BF)], [wide], (own_ref,), (mine, back), 16,
+    )
+    grad_input = grad_input.reshape(density.shape)
     partner = lax.ppermute(total, AXES, twin)
     scale = 1.0 / math.sqrt(float(extent_x * extent_y * extent_z * own_size * space_size))
     half = channels // 2

time: 73 us -> 72.6 us (level)
  starting transfers between devices: 11.5 us -> 15.4 us
  other arithmetic: 1.86 us -> 0.11 us
  local copies, waits for them, and re-layouts: 1.37 us -> 0.06 us
  Pallas kernels: 30.8 us -> 29.6 us
    ppermute x4, waiting for transfers between devices: 4.7 us -> 1.09 us  [shards(): pass_on = lambda value: lax.ppermute(value, AXES, onward)]
    ppermute x6 -> x5, waiting for transfers between devices: 11.2 us -> 14.3 us  [shards(): swap = lambda value: lax.ppermute(value, AXES, across)]
    ppermute x6 -> x5, starting transfers between devices: 10.9 us -> 12.7 us  [shards(): swap = lambda value: lax.ppermute(value, AXES, across)]
    transpose x1 -> x0, other arithmetic: 1.74 us -> none  [shards(): rows.transpose(2, 0, 1, 3)]
    ppermute x1, waiting for transfers between devices: 0.01 us -> 1.54 us  [shards(): total = parts[0] + lax.ppermute(parts[1], AXES, twin)]
    ppermute x1, waiting for transfers between devices: 1.36 us -> 0.01 us  [shards(): partner = lax.ppermute(total, AXES, twin)]
    ppermute x4, starting transfers between devices: 0.25 us -> 1.59 us  [shards(): pass_on = lambda value: lax.ppermute(value, AXES, onward)]
    pallas_call x9 -> x11, Pallas kernels: 30.8 us -> 29.6 us  [call(): pl.pallas_call(kernel, name=name, out_shape=[(pltpu.HBM if i < far_out el...]
  transfers between devices with their start and end apart: 15 -> 15, of which waited for: 10 -> 10; matrix products, arithmetic and copies ran while one was open for 3% -> 0% of each run, Pallas kernels for 28% -> 26%
where the time goes in v3:
time: 72.6 us; the launch traced here: 72.3 us
  Pallas kernels  29.6 us (41%)
  waiting for transfers between devices  26.4 us (36%)
  starting transfers between devices  15.4 us (21%)
  between operations  0.83 us (1%)
    pallas_call x11, Pallas kernels, call(): pl.pallas_call(kernel, name=name, out_shape=[(pltpu.HBM if i < far_out el...  29.6 us
    ppermute x5, waiting for transfers between devices, shards(): swap = lambda value: lax.ppermute(value, AXES, across)  14.3 us
    ppermute x5, starting transfers between devices, shards(): swap = lambda value: lax.ppermute(value, AXES, across)  12.7 us
    ppermute x3, waiting for transfers between devices, shards(): total = sent.astype(F32) + lax.ppermute(sent, AXES, pairs).astype(F32)  8.67 us
    ppermute x4, starting transfers between devices, shards(): pass_on = lambda value: lax.ppermute(value, AXES, onward)  1.59 us
    ppermute x1, waiting for transfers between devices, shards(): total = parts[0] + lax.ppermute(parts[1], AXES, twin)  1.54 us
  transfers between devices with their start and end apart: 15, of which 10 were waited for; matrix products, arithmetic and copies ran while one was open for 0% of the time, Pallas kernels for 26%

profile of v3, /device:TPU:0, one launch (start us, length us, event | category | flops | bytes accessed | tf_op | source)
XLA Modules:
  0.0 72.3 jit_solution(16400396638691038975)
XLA Ops:
  0.6 1.5 %density.1 = (bf16[8,256,128]{2,1,0:T(8,128)(2,1)S(1)}, bf16[1088,128]{1,0:T(8,128)(2,1)S(1)}, bf16[1024,128]{1,0:T(8,128)(2,1)S(1)}, bf16[1280,128]{1,0:T(8,128)(2,1)S(1)}, bf16[512,128]{1,0:T(8,128)(2,1)S(1)}) custom-call(s32[1]{0:T(128)} %bitcast.own_ref, s32[1]{0:T(128)} %bitcast.1.core_ref.refs_0_, bf16[256,8,128]{2,1,0:T(8,128)(2,1)} %bitcast.14, ...), custom_call_target="tpu_custom_call" | custom-call | flops 1150000000 | bytes 1024 | tf_op jit(solution)/shard_map/density/pallas_call | solution.py:389
  2.1 3.0 %collective-permute-start = (bf16[1088,128]{1,0:T(8,128)(2,1)S(1)}, bf16[1088,128]{1,0:T(8,128)(2,1)S(1)}, u32[]{:S(2)}, u32[]{:S(2)}) collective-permute-start(bf16[1088,128]{1,0:T(8,128)(2,1)S(1)} %get-tuple-element.48.mine), channel_id=1, source_target_pairs={{0,16},{1,17},{2,18},{3,19},{4,20},{5,21},{6,22},{7,23},{8,24},{9,... | collective-permute-start | bytes 835592 | tf_op jit(solution)/shard_map/ppermute | solution.py:410
  5.1 1.3 %cotangent.1 = (bf16[8,256,128]{2,1,0:T(8,128)(2,1)S(1)}, bf16[2304,128]{1,0:T(8,128)(2,1)S(1)}, bf16[1024,128]{1,0:T(8,128)(2,1)S(1)}) custom-call(s32[1]{0:T(128)} %bitcast.own_ref, bf16[256,8,128]{2,1,0:T(8,128)(2,1)} %bitcast.15, bf16[1280,128]{1,0:T(8,128)(2,1)S(1)} %get-tuple-element.49.more), custom_call_target="tpu_custom_call" | custom-call | flops 1150000000 | bytes 1024 | tf_op jit(solution)/shard_map/cotangent/pallas_call | solution.py:389
  6.5 0.1 collective-permute-start.2
  6.6 0.1 collective-permute-start.5
  6.6 6.0 %collective-permute-done.message.rest = bf16[1088,128]{1,0:T(8,128)(2,1)S(1)} collective-permute-done((bf16[1088,128]{1,0:T(8,128)(2,1)S(1)}, bf16[1088,128]{1,0:T(8,128)(2,1)S(1)}, u32[]{:S(2)}, u32[]{:S(2)}) %collective-permute-start) | collective-permute-done | bytes 278560 | tf_op jit(solution)/shard_map/ppermute | solution.py:410
  12.6 0.0 collective-permute-start.6
  12.6 4.0 %collective-permute-start.1 = (bf16[1024,128]{1,0:T(8,128)(2,1)S(1)}, bf16[1024,128]{1,0:T(8,128)(2,1)S(1)}, u32[]{:S(2)}, u32[]{:S(2)}) collective-permute-start(bf16[1024,128]{1,0:T(8,128)(2,1)S(1)} %get-tuple-element.62), channel_id=1, source_target_pairs={{0,16},{1,17},{2,18},{3,19},{4,20},{5,21},{6,22},{7,23},{8,24},{9,... | collective-permute-start | bytes 786440 | tf_op jit(solution)/shard_map/ppermute | solution.py:410
  16.6 4.3 %stencils.1 = (bf16[16,128,768]{2,1,0:T(8,128)(2,1)}, bf16[16,128,768]{2,1,0:T(8,128)(2,1)}, bf16[16,128,768]{2,1,0:T(8,128)(2,1)S(1)}, bf16[16,128,768]{2,1,0:T...) custom-call(s32[1]{0:T(128)} %bitcast.own_ref, ...), custom_call_target="tpu_custom_call" | custom-call | flops 5750000128 | bytes 1024 | tf_op jit(solution)/shard_map/stencils/pallas_call | solution.py:389
  21.0 4.3 %collective-permute-done.2.beside = bf16[2304,128]{1,0:T(8,128)(2,1)S(1)} collective-permute-done((bf16[2304,128]{1,0:T(8,128)(2,1)S(1)}, bf16[2304,128]{1,0:T(8,128)(2,1)S(1)}, u32[]{:S(2)}, u32[]{:S(2)}) %collective-permute-start.2) | collective-permute-done | bytes 589856 | tf_op jit(solution)/shard_map/ppermute | solution.py:410
  25.3 0.0 collective-permute-start.7
  25.3 0.5 collective-permute-start.3
  25.8 0.7 collective-permute-done.7.twin
  26.5 1.0 %collective-permute-start.4 = (bf16[1024,128]{1,0:T(8,128)(2,1)S(1)}, bf16[1024,128]{1,0:T(8,128)(2,1)S(1)}, u32[]{:S(2)}, u32[]{:S(2)}) collective-permute-start(bf16[1024,128]{1,0:T(8,128)(2,1)S(1)} %slice.12.rest), channel_id=1, source_target_pairs={{0,1},{1,2},{2,3},{3,4},{4,5},{5,6},{6,7},{7,8},{8,9},{9,10},{10,1... | collective-permute-start | bytes 786440 | tf_op jit(solution)/shard_map/ppermute | solution.py:411
  27.6 0.1 weights.1
  27.7 0.0 collective-permute-done.5.halo
  27.7 0.0 collective-permute-done.6.halo_beside
  27.7 2.9 %forward.1 = (bf16[24,256,128]{2,1,0:T(8,128)(2,1)S(1)}, bf16[16,256,128]{2,1,0:T(8,128)(2,1)S(1)}, bf16[16,256,128]{2,1,0:T(8,128)(2,1)S(1)}, bf16[16,256,128]{2,1,0:T(8,128)(2,1)S(1)}) custom-call(s32[1]{0:T(128)} %bitcast.own_ref, bf16[8,256,128]{2,1,0:T(8,128)(2,1)S(1)} %get-tuple-element.63.local, bf16[2304,128]{1,0:T(8,128)(2,1)S(1)} %collective-permute-done.2.beside, ...), custom_call_target="tpu_custom_call" | custom-call | bytes 1024 | tf_op jit(solution)/shard_map/forward/pallas_call | solution.py:389
  30.6 1.6 %later.1.second = bf16[8,256,128]{2,1,0:T(8,128)(2,1)S(1)} custom-call(bf16[16,256,128]{2,1,0:T(8,128)(2,1)S(1)} %get-tuple-element.75.act, bf16[16,128,768]{2,1,0:T(8,128)(2,1)S(1)} %get-tuple-element.76.two_forward, bf16[128,256]{1,0:T(8,128)(2,1)S(1)} %get-tuple-element.66.turn), custom_call_target="tpu_custom_call" | custom-call | bytes 1024 | tf_op jit(solution)/shard_map/later/pallas_call | solution.py:389
  32.2 0.0 collective-permute-done.1.beside
  32.2 4.0 %second.1 = (f32[256,256]{1,0:T(8,128)S(1)}, f32[256,128]{1,0:T(8,128)S(1)}) custom-call(s32[1]{0:T(128)} %bitcast.own_ref, bf16[16,256,128]{2,1,0:T(8,128)(2,1)S(1)} %get-tuple-element.75.act, bf16[8,256,128]{2,1,0:T(8,128)(2,1)S(1)} %later.1.second, bf16[8,256,128]{2,1,0:T(8,128)(2,1)S(1)} %get-tuple-element.53.local, ...), custom_call_target="tpu_custom_call" | custom-call | flops 4600000000 | bytes 1024 | tf_op jit(solution)/shard_map/second/pallas_call | solution.py:389
  36.2 0.0 collective-permute-done.3.halo
  36.2 1.1 %collective-permute-done.4.halo_beside = bf16[1024,128]{1,0:T(8,128)(2,1)S(1)} collective-permute-done((bf16[1024,128]{1,0:T(8,128)(2,1)S(1)}, bf16[1024,128]{1,0:T(8,128)(2,1)S(1)}, u32[]{:S(2)}, u32[]{:S(2)}) %collective-permute-start.4) | collective-permute-done | bytes 262176 | tf_op jit(solution)/shard_map/ppermute | solution.py:411
  37.3 8.5 %backward.1 = (bf16[16,256,128]{2,1,0:T(8,128)(2,1)S(1)}, f32[2,2,144,256]{3,2,1,0:T(8,128)S(1)}) custom-call(s32[1]{0:T(128)} %bitcast.own_ref, s32[1]{0:T(128)} %bitcast.1.core_ref.refs_0_, bf16[16,128,768]{2,1,0:T(8,128)(2,1)} %get-tuple-element.55.two_source, bf16[8,256,128]{2,1,0:T(8,128)(2,1)S(1)} %get-tuple-element.53.local, ...), custom_call_target="tpu_custom_call" | custom-call | flops 9200000000 | bytes 1024 | tf_op jit(solution)/shard_map/backward/pallas_call | solution.py:389
  45.9 0.1 collective-permute-start.8
  46.0 1.5 %collective-permute-done.8 = f32[2,144,256]{2,1,0:T(8,128)S(1)} collective-permute-done((f32[2,144,256]{2,1,0:T(8,128)S(1)}, f32[2,144,256]{2,1,0:T(8,128)S(1)}, u32[]{:S(2)}, u32[]{:S(2)}) %collective-permute-start.8) | collective-permute-done | bytes 294944 | tf_op jit(solution)/shard_map/ppermute | solution.py:489
  47.6 4.3 %collective-permute-start.9 = (bf16[144,256]{1,0:T(8,128)(2,1)S(1)}, bf16[144,256]{1,0:T(8,128)(2,1)S(1)}, u32[]{:S(2)}, u32[]{:S(2)}) collective-permute-start(bf16[144,256]{1,0:T(8,128)(2,1)S(1)} %fusion), channel_id=1, source_target_pairs={{0,16},{1,17},{2,18},{3,19},{4,20},{5,21},{6,22},{7,23},{8,24},{9,... | collective-permute-start | bytes 221192 | tf_op jit(solution)/shard_map/ppermute | solution.py:410
  51.9 2.6 %collective-permute-done.9 = bf16[144,256]{1,0:T(8,128)(2,1)S(1)} collective-permute-done((bf16[144,256]{1,0:T(8,128)(2,1)S(1)}, bf16[144,256]{1,0:T(8,128)(2,1)S(1)}, u32[]{:S(2)}, u32[]{:S(2)}) %collective-permute-start.9) | collective-permute-done | bytes 73760 | tf_op jit(solution)/shard_map/ppermute | solution.py:410
  54.5 0.1 collective-permute-start.10
  54.6 3.5 %input.1 = (bf16[4,256,128]{2,1,0:T(8,128)(2,1)S(1)}, bf16[4,256,128]{2,1,0:T(8,128)(2,1)S(1)}) custom-call(s32[1]{0:T(128)} %bitcast.own_ref, bf16[16,128,768]{2,1,0:T(8,128)(2,1)} %get-tuple-element.52.one_source, bf16[8,256,128]{2,1,0:T(8,128)(2,1)S(1)} %get-tuple-element.53.local, bf16[1024,128]{1,0:T(8,128)(2,1)S(1)} %collective-permute-done.1.beside, ...), custom_call_target="tpu_custom_call" | custom-call | flops 3449999872 | bytes 1024 | tf_op jit(solution)/shard_map/input/pallas_call | solution.py:389
  58.1 0.8 %collective-permute-done.10 = bf16[144,256]{1,0:T(8,128)(2,1)S(1)} collective-permute-done((bf16[144,256]{1,0:T(8,128)(2,1)S(1)}, bf16[144,256]{1,0:T(8,128)(2,1)S(1)}, u32[]{:S(2)}, u32[]{:S(2)}) %collective-permute-start.10) | collective-permute-done | bytes 73760 | tf_op jit(solution)/shard_map/ppermute | solution.py:510
  58.9 0.1 collective-permute-start.12
  59.0 4.3 %collective-permute-done.12 = bf16[144,256]{1,0:T(8,128)(2,1)S(1)} collective-permute-done((bf16[144,256]{1,0:T(8,128)(2,1)S(1)}, bf16[144,256]{1,0:T(8,128)(2,1)S(1)}, u32[]{:S(2)}, u32[]{:S(2)}) %collective-permute-start.12) | collective-permute-done | bytes 73760 | tf_op jit(solution)/shard_map/ppermute | solution.py:510
  63.4 0.8 %collective-permute-start.13 = (bf16[144,256]{1,0:T(8,128)(2,1)S(1)}, bf16[144,256]{1,0:T(8,128)(2,1)S(1)}, u32[]{:S(2)}, u32[]{:S(2)}) collective-permute-start(bf16[144,256]{1,0:T(8,128)(2,1)S(1)} %add_convert_fusion), channel_id=1, source_target_pairs={{0,8},{1,9},{2,10},{3,11},{4,12},{5,13},{6,14},{7,15},{8,0},{9,1},... | collective-permute-start | bytes 221192 | tf_op jit(solution)/shard_map/ppermute | solution.py:510
  64.2 1.3 %collective-permute-start.11 = (bf16[4,256,128]{2,1,0:T(8,128)(2,1)S(1)}, bf16[4,256,128]{2,1,0:T(8,128)(2,1)S(1)}, u32[]{:S(2)}, u32[]{:S(2)}) collective-permute-start(bf16[4,256,128]{2,1,0:T(8,128)(2,1)S(1)} %get-tuple-element.85), channel_id=1, source_target_pairs={{0,16},{1,17},{2,18},{3,19},{4,20},{5,21},{6,22},{7,23},{8,24},{9,... | collective-permute-start | bytes 786440 | tf_op jit(solution)/shard_map/ppermute | solution.py:410
  65.4 3.5 %collective-permute-done.13 = bf16[144,256]{1,0:T(8,128)(2,1)S(1)} collective-permute-done((bf16[144,256]{1,0:T(8,128)(2,1)S(1)}, bf16[144,256]{1,0:T(8,128)(2,1)S(1)}, u32[]{:S(2)}, u32[]{:S(2)}) %collective-permute-start.13) | collective-permute-done | bytes 73760 | tf_op jit(solution)/shard_map/ppermute | solution.py:510
  69.0 0.1 collective-permute-start.14
  69.0 1.5 %collective-permute-done.11.back = bf16[4,256,128]{2,1,0:T(8,128)(2,1)S(1)} collective-permute-done((bf16[4,256,128]{2,1,0:T(8,128)(2,1)S(1)}, bf16[4,256,128]{2,1,0:T(8,128)(2,1)S(1)}, u32[]{:S(2)}, u32[]{:S(2)}) %collective-permute-start.11) | collective-permute-done | bytes 262176 | tf_op jit(solution)/shard_map/ppermute | solution.py:410
  70.5 1.1 %assemble.1 = bf16[256,8,128]{2,1,0:T(8,128)(2,1)} custom-call(s32[1]{0:T(128)} %bitcast.own_ref, bf16[4,256,128]{2,1,0:T(8,128)(2,1)S(1)} %get-tuple-element.82.mine, bf16[4,256,128]{2,1,0:T(8,128)(2,1)S(1)} %collective-permute-done.11.back), custom_call_target="tpu_custom_call" | custom-call | bytes 1024 | tf_op jit(solution)/shard_map/assemble/pallas_call | solution.py:389
  71.6 0.0 collective-permute-done.14.refs_2_
  71.6 0.7 %finish.1 = (f32[128,256]{1,0:T(8,128)}, f32[128,256]{1,0:T(8,128)}, f32[27,128]{1,0:T(8,128)}, f32[27,128]{1,0:T(8,128)}) custom-call(s32[1]{0:T(128)} %bitcast.1.core_ref.refs_0_, f32[144,256]{1,0:T(8,128)S(1)} %convert_add_fusion.refs_1_, f32[144,256]{1,0:T(8,128)S(1)} %collective-permute-done.14.refs_2_), custom_call_target="tpu_custom_call" | custom-call | flops 1150000000 | bytes 1024 | tf_op jit(solution)/shard_map/finish/pallas_call | solution.py:389
  (9 shorter events, 0.2 us)
Async XLA Ops:
  2.1 10.5 %collective-permute-start = (bf16[1088,128]{1,0:T(8,128)(2,1)S(1)}, bf16[1088,128]{1,0:T(8,128)(2,1)S(1)}, u32[]{:S(2)}, u32[]{:S(2)}) collective-permute-start(bf16[1088,128]{1,0:T(8,128)(2,1)S(1)} %get-tuple-element.48.mine), channel_id=1, source_target_pairs={{0,16},{1,17},{2,18},{3,19},{4,20},{5,21},{6,22},{7,23},{8,24},{9,... | collective-permute-start | bytes 835592 | tf_op jit(solution)/shard_map/ppermute | solution.py:410
  6.5 18.8 %collective-permute-start.2 = (bf16[2304,128]{1,0:T(8,128)(2,1)S(1)}, bf16[2304,128]{1,0:T(8,128)(2,1)S(1)}, u32[]{:S(2)}, u32[]{:S(2)}) collective-permute-start(bf16[2304,128]{1,0:T(8,128)(2,1)S(1)} %get-tuple-element.58), channel_id=1, source_target_pairs={{0,16},{1,17},{2,18},{3,19},{4,20},{5,21},{6,22},{7,23},{8,24},{9,... | collective-permute-start | bytes 1769480 | tf_op jit(solution)/shard_map/ppermute | solution.py:410
  6.6 21.1 %collective-permute-start.5 = (bf16[1024,128]{1,0:T(8,128)(2,1)S(1)}, bf16[1024,128]{1,0:T(8,128)(2,1)S(1)}, u32[]{:S(2)}, u32[]{:S(2)}) collective-permute-start(bf16[1024,128]{1,0:T(8,128)(2,1)S(1)} %get-tuple-element.64), channel_id=1, source_target_pairs={{0,1},{1,2},{2,3},{3,4},{4,5},{5,6},{6,7},{7,8},{8,9},{9,10},{10,1... | collective-permute-start | bytes 786440 | tf_op jit(solution)/shard_map/ppermute | solution.py:411
  12.6 15.1 %collective-permute-start.6 = (bf16[1088,128]{1,0:T(8,128)(2,1)S(1)}, bf16[1088,128]{1,0:T(8,128)(2,1)S(1)}, u32[]{:S(2)}, u32[]{:S(2)}) collective-permute-start(bf16[1088,128]{1,0:T(8,128)(2,1)S(1)} %collective-permute-done.message.rest), channel_id=1, source_target_pairs={{0,1},{1,2},{2,3},{3,4},{4,5},{5,6},{6,7},{7,8},{8,9},{9,10},{10,1... | collective-permute-start | bytes 835592 | tf_op jit(solution)/shard_map/ppermute | solution.py:411
  12.6 19.6 %collective-permute-start.1 = (bf16[1024,128]{1,0:T(8,128)(2,1)S(1)}, bf16[1024,128]{1,0:T(8,128)(2,1)S(1)}, u32[]{:S(2)}, u32[]{:S(2)}) collective-permute-start(bf16[1024,128]{1,0:T(8,128)(2,1)S(1)} %get-tuple-element.62), channel_id=1, source_target_pairs={{0,16},{1,17},{2,18},{3,19},{4,20},{5,21},{6,22},{7,23},{8,24},{9,... | collective-permute-start | bytes 786440 | tf_op jit(solution)/shard_map/ppermute | solution.py:410
  25.3 1.3 %collective-permute-start.7 = (bf16[256,128]{1,0:T(8,128)(2,1)S(1)}, bf16[256,128]{1,0:T(8,128)(2,1)S(1)}, u32[]{:S(2)}, u32[]{:S(2)}) collective-permute-start(bf16[256,128]{1,0:T(8,128)(2,1)S(1)} %slice.13.beside), channel_id=1, source_target_pairs={{0,1},{1,0},{2,3},{3,2},{4,5},{5,4},{6,7},{7,6},{8,9},{9,8},{10,11... | collective-permute-start | bytes 196616 | tf_op jit(solution)/shard_map/ppermute | solution.py:458
  25.3 10.9 %collective-permute-start.3 = (bf16[1024,128]{1,0:T(8,128)(2,1)S(1)}, bf16[1024,128]{1,0:T(8,128)(2,1)S(1)}, u32[]{:S(2)}, u32[]{:S(2)}) collective-permute-start(bf16[1024,128]{1,0:T(8,128)(2,1)S(1)} %get-tuple-element.62), channel_id=1, source_target_pairs={{0,1},{1,2},{2,3},{3,4},{4,5},{5,6},{6,7},{7,8},{8,9},{9,10},{10,1... | collective-permute-start | bytes 786440 | tf_op jit(solution)/shard_map/ppermute | solution.py:411
  26.5 10.8 %collective-permute-start.4 = (bf16[1024,128]{1,0:T(8,128)(2,1)S(1)}, bf16[1024,128]{1,0:T(8,128)(2,1)S(1)}, u32[]{:S(2)}, u32[]{:S(2)}) collective-permute-start(bf16[1024,128]{1,0:T(8,128)(2,1)S(1)} %slice.12.rest), channel_id=1, source_target_pairs={{0,1},{1,2},{2,3},{3,4},{4,5},{5,6},{6,7},{7,8},{8,9},{9,10},{10,1... | collective-permute-start | bytes 786440 | tf_op jit(solution)/shard_map/ppermute | solution.py:411
  45.9 1.6 %collective-permute-start.8 = (f32[2,144,256]{2,1,0:T(8,128)S(1)}, f32[2,144,256]{2,1,0:T(8,128)S(1)}, u32[]{:S(2)}, u32[]{:S(2)}) collective-permute-start(f32[2,144,256]{2,1,0:T(8,128)S(1)} %slice_bitcast_fusion), channel_id=1, source_target_pairs={{0,1},{1,0},{2,3},{3,2},{4,5},{5,4},{6,7},{7,6},{8,9},{9,8},{10,11... | collective-permute-start | bytes 884744 | tf_op jit(solution)/shard_map/ppermute | solution.py:489
  47.6 6.9 %collective-permute-start.9 = (bf16[144,256]{1,0:T(8,128)(2,1)S(1)}, bf16[144,256]{1,0:T(8,128)(2,1)S(1)}, u32[]{:S(2)}, u32[]{:S(2)}) collective-permute-start(bf16[144,256]{1,0:T(8,128)(2,1)S(1)} %fusion), channel_id=1, source_target_pairs={{0,16},{1,17},{2,18},{3,19},{4,20},{5,21},{6,22},{7,23},{8,24},{9,... | collective-permute-start | bytes 221192 | tf_op jit(solution)/shard_map/ppermute | solution.py:410
  54.5 4.4 %collective-permute-start.10 = (bf16[144,256]{1,0:T(8,128)(2,1)S(1)}, bf16[144,256]{1,0:T(8,128)(2,1)S(1)}, u32[]{:S(2)}, u32[]{:S(2)}) collective-permute-start(bf16[144,256]{1,0:T(8,128)(2,1)S(1)} %bitcast_add_fusion.1), channel_id=1, source_target_pairs={{0,2},{1,5},{2,0},{3,7},{4,6},{5,1},{6,4},{7,3},{8,10},{9,13},{10,... | collective-permute-start | bytes 221192 | tf_op jit(solution)/shard_map/ppermute | solution.py:510
  58.9 4.4 %collective-permute-start.12 = (bf16[144,256]{1,0:T(8,128)(2,1)S(1)}, bf16[144,256]{1,0:T(8,128)(2,1)S(1)}, u32[]{:S(2)}, u32[]{:S(2)}) collective-permute-start(bf16[144,256]{1,0:T(8,128)(2,1)S(1)} %add_convert_fusion.1), channel_id=1, source_target_pairs={{0,4},{1,3},{2,6},{3,1},{4,0},{5,7},{6,2},{7,5},{8,12},{9,11},{10,... | collective-permute-start | bytes 221192 | tf_op jit(solution)/shard_map/ppermute | solution.py:510
  63.4 5.5 %collective-permute-start.13 = (bf16[144,256]{1,0:T(8,128)(2,1)S(1)}, bf16[144,256]{1,0:T(8,128)(2,1)S(1)}, u32[]{:S(2)}, u32[]{:S(2)}) collective-permute-start(bf16[144,256]{1,0:T(8,128)(2,1)S(1)} %add_convert_fusion), channel_id=1, source_target_pairs={{0,8},{1,9},{2,10},{3,11},{4,12},{5,13},{6,14},{7,15},{8,0},{9,1},... | collective-permute-start | bytes 221192 | tf_op jit(solution)/shard_map/ppermute | solution.py:510
  64.2 6.4 %collective-permute-start.11 = (bf16[4,256,128]{2,1,0:T(8,128)(2,1)S(1)}, bf16[4,256,128]{2,1,0:T(8,128)(2,1)S(1)}, u32[]{:S(2)}, u32[]{:S(2)}) collective-permute-start(bf16[4,256,128]{2,1,0:T(8,128)(2,1)S(1)} %get-tuple-element.85), channel_id=1, source_target_pairs={{0,16},{1,17},{2,18},{3,19},{4,20},{5,21},{6,22},{7,23},{8,24},{9,... | collective-permute-start | bytes 786440 | tf_op jit(solution)/shard_map/ppermute | solution.py:410
  69.0 2.6 %collective-permute-start.14 = (f32[144,256]{1,0:T(8,128)S(1)}, f32[144,256]{1,0:T(8,128)S(1)}, u32[]{:S(2)}, u32[]{:S(2)}) collective-permute-start(f32[144,256]{1,0:T(8,128)S(1)} %convert_add_fusion.refs_1_), channel_id=1, source_target_pairs={{0,1},{1,0},{2,3},{3,2},{4,5},{5,4},{6,7},{7,6},{8,9},{9,8},{10,11... | collective-permute-start | bytes 442376 | tf_op jit(solution)/shard_map/ppermute | solution.py:515
